TPU v7x, 512 devices: a whole 4x8x8 slice. The times are simulated.
512 devices in a mesh: grp: 16 (over y, core), ta: 4 (over z_hi), ha: 8 (over x, z_lo).
Axes of the slice: x: 4, y: 8, z: 8 (z_hi: 4, z_lo: 2; z = z_hi * 2 + z_lo), core: 2. Of those that a mesh axis runs over, the one named last changes fastest.
Arguments:
- queries: bfloat16 [64, 8, 128, 1536], P(('grp', 'ta'), 'ha'), parts along dimension 0, may hold values from -6 to 6
- key_tiles: bfloat16 [64, 8, 128, 1536], P(('grp', 'ta'), 'ha'), parts along dimension 0, may hold values from -6 to 6
- value_tiles: bfloat16 [64, 8, 128, 1536], P(('grp', 'ta'), 'ha'), parts along dimension 0, may hold values from -6 to 6
- outputs: bfloat16 [64, 8, 128, 1536], P(('grp', 'ta'), 'ha'), parts along dimension 0, may hold values from -6 to 6
- grads_out: bfloat16 [64, 8, 128, 1536], P(('grp', 'ta'), 'ha'), parts along dimension 0, may hold values from -6 to 6
- log_sums: float32 [64, 8, 12, 128], P(('grp', 'ta'), 'ha'), parts along dimension 0, may hold values from 4 to 7
- tile_counts: int32 [64, 8], P('grp'), parts along dimension 0, may hold values from 32 to 128, as said below
- head_reach: int32 [12, 2], replicated, may hold values from 0 to 1, as said below
Outputs:
- query_grads: bfloat16 [64, 8, 128, 1536], P(('grp', 'ta'), 'ha'), parts along dimension 0
- key_grads: bfloat16 [64, 8, 128, 1536], P(('grp', 'ta'), 'ha'), parts along dimension 0
- value_grads: bfloat16 [64, 8, 128, 1536], P(('grp', 'ta'), 'ha'), parts along dimension 0
There are 16 independent parts, one for each index of `grp`. A program takes and returns all parts, laid end to end along the dimension named above; an argument that names none is the same for every part. Nothing has to cross between parts.
Inputs may be any that keep to these rules, and one draw needn't show every extreme that they name: `tile_counts`: tiles outside the last time row and the last height column hold all 128 tokens; the tile in the last row and last column holds 32. `head_reach`: some head reaches 1 along both axes and some head 0 along both.
All inputs are finite; a program needn't handle non-finite values.
Results may differ from a plain program's by a relative error of at most 0.0057.
Values may be sent and summed in bfloat16 or wider, within the bound.
A program may use at most 128 MiB of HBM per device.

v0:
```python
import jax
import jax.numpy as jnp
from jax import lax
from jax.sharding import PartitionSpec as P

HEADS = 12
HEAD_DIM = 128


def passed_along(block, axis, distance):
    devices = range(lax.axis_size(axis))
    route = [(i - distance, i) for i in devices if i - distance in devices]
    return lax.ppermute(block, axis, route)


def with_halo(block, sides, width):
    for axis, dim in sides:
        count = lax.axis_size(axis)
        forward = [(i, i + 1) for i in range(count - 1)]
        backward = [(target, source) for source, target in forward]
        low = lax.ppermute(
            lax.slice_in_dim(block, block.shape[dim] - width, None, axis=dim), axis, forward
        )
        high = lax.ppermute(lax.slice_in_dim(block, 0, width, axis=dim), axis, backward)
        block = jnp.concatenate([low, block, high], axis=dim)
    return block


def slot_allowed(head_reach):
    slot_ids = jnp.arange(9)
    step_t = jnp.abs(slot_ids // 3 - 1)
    step_h = jnp.abs(slot_ids % 3 - 1)
    return (step_t[None, :] <= head_reach[:, 0:1]) & (step_h[None, :] <= head_reach[:, 1:2])


def heads_first(tiles):
    return jnp.transpose(tiles.reshape(-1, HEADS, HEAD_DIM), (1, 0, 2))


def attend_back(
    query_rows, grad_rows, lse_rows, delta_rows, key_rows, value_rows, row_mask, col_mask
):
    score_scale = HEAD_DIM ** (-0.5)
    scores = (
        jnp.einsum("hrd,hcd->hrc", query_rows, key_rows, preferred_element_type=jnp.float32)
        * score_scale
    )
    visible = row_mask[:, :, None] & col_mask[:, None, :]
    soft_probs = jnp.where(visible, jnp.exp(scores - lse_rows[:, :, None]), jnp.float32(0.0))
    dprobs = jnp.einsum("hrd,hcd->hrc", grad_rows, value_rows, preferred_element_type=jnp.float32)
    score_grads = (soft_probs * (dprobs - delta_rows[:, :, None]) * score_scale).astype(
        jnp.bfloat16
    )
    return (soft_probs.astype(jnp.bfloat16), score_grads)


def send_height(piece, step):
    return passed_along(piece, "ha", step)


def send_time(piece, step):
    return passed_along(piece, "ta", step)


def route_parts(grad_parts, axis_dim, sender):
    lower_part = jnp.take(grad_parts, 0, axis=axis_dim)
    middle = jnp.take(grad_parts, 1, axis=axis_dim)
    upper_part = jnp.take(grad_parts, 2, axis=axis_dim)
    return (sender(upper_part, 1), middle, sender(lower_part, -1))


def add_pieces(pieces):
    total = pieces[0].astype(jnp.float32)
    for piece in pieces[1:]:
        total = total + piece.astype(jnp.float32)
    return total


def tokens_first(head_major, tok_rows, feat_width):
    return jnp.transpose(head_major, (1, 0, 2)).reshape(1, 1, tok_rows, feat_width)


def per_device(
    queries, key_tiles, value_tiles, outputs, grads_out, log_sums, tile_counts, head_reach
):
    tok_rows = queries.shape[2]
    feat_width = queries.shape[3]
    place_t = lax.axis_index("ta")
    place_h = lax.axis_index("ha")
    near_counts = lax.dynamic_slice(jnp.pad(tile_counts, 1), (place_t, place_h), (3, 3)).reshape(9)
    near_live = jnp.arange(tok_rows)[None, :] < near_counts[:, None]
    own_live = jnp.arange(tok_rows) < near_counts[4]
    allowed = slot_allowed(head_reach)
    key_mask = (allowed[:, :, None] & near_live[None]).reshape(HEADS, 9 * tok_rows)
    query_head = heads_first(queries[0, 0])
    grad_head = heads_first(grads_out[0, 0])
    out_head = heads_first(outputs[0, 0])
    row_delta = jnp.sum(grad_head.astype(jnp.float32) * out_head.astype(jnp.float32), axis=2)
    near_keys, near_values = (
        with_halo(key_tiles, (("ta", 0), ("ha", 1)), 1),
        with_halo(value_tiles, (("ta", 0), ("ha", 1)), 1),
    )
    key_head = heads_first(near_keys)
    value_head = heads_first(near_values)
    soft_probs, score_grads = attend_back(
        query_head,
        grad_head,
        log_sums[0, 0],
        row_delta,
        key_head,
        value_head,
        own_live[None, :],
        key_mask,
    )
    dquery = jnp.einsum(
        "hrc,hcd->hrd", score_grads, key_head, preferred_element_type=jnp.float32
    ).astype(jnp.bfloat16)
    query_grads = tokens_first(dquery, tok_rows, feat_width)
    dkey_part = jnp.einsum(
        "hrc,hrd->hcd", score_grads, query_head, preferred_element_type=jnp.float32
    ).astype(jnp.bfloat16)
    dval_part = jnp.einsum(
        "hrc,hrd->hcd", soft_probs, grad_head, preferred_element_type=jnp.float32
    ).astype(jnp.bfloat16)
    grad_parts = lax.optimization_barrier(
        jnp.stack([dkey_part, dval_part]).reshape(2, HEADS, 3, 3, tok_rows, HEAD_DIM)
    )
    first_hop = route_parts(grad_parts, 3, send_height)
    regrouped = jnp.stack(first_hop, axis=3)
    grad_total = jnp.sum(add_pieces(route_parts(regrouped, 2, send_time)), axis=2)
    grad_total = grad_total.astype(jnp.bfloat16)
    key_grads = tokens_first(grad_total[0], tok_rows, feat_width)
    value_grads = tokens_first(grad_total[1], tok_rows, feat_width)
    return (query_grads, key_grads, value_grads)


def solution(mesh):
    in_specs = (
        P(("grp", "ta"), "ha", None, None),
        P(("grp", "ta"), "ha", None, None),
        P(("grp", "ta"), "ha", None, None),
        P(("grp", "ta"), "ha", None, None),
        P(("grp", "ta"), "ha", None, None),
        P(("grp", "ta"), "ha", None, None),
        P("grp", None),
        P(),
    )
    out_specs = (
        P(("grp", "ta"), "ha", None, None),
        P(("grp", "ta"), "ha", None, None),
        P(("grp", "ta"), "ha", None, None),
    )
    return jax.shard_map(
        per_device, mesh=mesh, in_specs=in_specs, out_specs=out_specs, check_vma=False
    )
```

profile of v0, /device:TPU:1, one launch (start us, length us, event | category | flops | bytes accessed | tf_op | source)
XLA Modules:
  0.0 407.4 jit_solution(716622352540166630)
XLA Ops:
  0.6 6.8 %collective-permute-start = (bf16[1,1,128,1536]{3,2,1,0:T(8,128)(2,1)}, bf16[1,1,128,1536]{3,2,1,0:T(8,128)(2,1)S(1)}, u32[]{:S(2)}, u32[]{:S(2)}) collective-permute-start(bf16[1,1,128,1536]{3,2,1,0:T(8,128)(2,1)} %param.21), channel_id=1, source_target_pairs={{0,8},{8,16},{16,24},{1,9},{9,17},{17,25},{2,10},{10,18},{18,26},{... | collective-permute-start | bytes 1179656 | tf_op jit(solution)/shard_map/ppermute | solution.py:21
  7.4 1.3 collective-permute-start.1
  8.7 8.4 %collective-permute-start.4 = (bf16[1,1,128,1536]{3,2,1,0:T(8,128)(2,1)}, bf16[1,1,128,1536]{3,2,1,0:T(8,128)(2,1)}, u32[]{:S(2)}, u32[]{:S(2)}) collective-permute-start(bf16[1,1,128,1536]{3,2,1,0:T(8,128)(2,1)} %param.22), channel_id=1, source_target_pairs={{0,8},{8,16},{16,24},{1,9},{9,17},{17,25},{2,10},{10,18},{18,26},{... | collective-permute-start | bytes 1179656 | tf_op jit(solution)/shard_map/ppermute | solution.py:21
  17.1 1.3 collective-permute-start.5
  18.5 0.8 pad_dynamic-slice_fusion
  19.2 0.1 reshape.161
  19.3 0.6 slice.19
  19.9 0.1 broadcast_reduce_fusion
  20.0 0.8 slice_bitcast_fusion.9
  20.8 0.1 compare_and_fusion
  20.9 1.0 constant_dynamic-update-slice_fusion.1
  21.9 18.3 %collective-permute-done.1 = bf16[1,1,128,1536]{3,2,1,0:T(8,128)(2,1)S(1)} collective-permute-done((bf16[1,1,128,1536]{3,2,1,0:T(8,128)(2,1)}, bf16[1,1,128,1536]{3,2,1,0:T(8,128)(2,1)S(1)}, u32[]{:S(2)}, u32[]{:S(2)}) %collective-permute-start.1) | collective-permute-done | bytes 393248 | tf_op jit(solution)/shard_map/ppermute | solution.py:24
  40.2 1.3 collective-permute-start.3
  41.5 5.0 %collective-permute-start.2 = (bf16[3,1,128,1536]{3,2,1,0:T(8,128)(2,1)S(1)}, bf16[3,1,128,1536]{3,2,1,0:T(8,128)(2,1)}, u32[]{:S(2)}, u32[]{:S(2)}) collective-permute-start(bf16[3,1,128,1536]{3,2,1,0:T(8,128)(2,1)S(1)} %constant_dynamic-update-slice_fusion), channel_id=1, source_target_pairs={{0,1},{1,2},{2,3},{3,4},{4,5},{5,6},{6,7},{8,9},{9,10},{10,11},{11... | collective-permute-start | bytes 3538952 | tf_op jit(solution)/shard_map/ppermute | solution.py:21
  46.5 1.8 constant_dynamic-update-slice_fusion.5
  48.3 1.8 constant_dynamic-update-slice_fusion.4
  50.1 0.8 constant_dynamic-update-slice_fusion.3
  50.9 1.3 collective-permute-start.7
  52.1 5.0 %collective-permute-start.6 = (bf16[3,1,128,1536]{3,2,1,0:T(8,128)(2,1)}, bf16[3,1,128,1536]{3,2,1,0:T(8,128)(2,1)}, u32[]{:S(2)}, u32[]{:S(2)}) collective-permute-start(bf16[3,1,128,1536]{3,2,1,0:T(8,128)(2,1)} %constant_dynamic-update-slice_fusion.3), channel_id=1, source_target_pairs={{0,1},{1,2},{2,3},{3,4},{4,5},{5,6},{6,7},{8,9},{9,10},{10,11},{11... | collective-permute-start | bytes 3538952 | tf_op jit(solution)/shard_map/ppermute | solution.py:21
  57.2 1.2 iota_compare_fusion
  58.4 0.6 copy.83
  59.0 0.1 and.67
  59.1 0.6 copy.69
  59.7 0.9 copy.40
  60.7 0.2 copy.45
  60.9 1.2 copy.43
  62.1 0.1 fusion.13
  62.3 1.3 broadcast_and_fusion
  63.6 11.2 %collective-permute-done.3 = bf16[3,1,128,1536]{3,2,1,0:T(8,128)(2,1)S(1)} collective-permute-done((bf16[3,1,128,1536]{3,2,1,0:T(8,128)(2,1)S(1)}, bf16[3,1,128,1536]{3,2,1,0:T(8,128)(2,1)S(1)}, u32[]{:S(2)}, u32[]{:S(2)}) %collective-permute-start.3) | collective-permute-done | bytes 1179680 | tf_op jit(solution)/shard_map/ppermute | solution.py:24
  74.8 1.0 copy-done.9
  75.8 2.2 pad_maximum_fusion.2
  78.0 4.4 %reshape.162 = bf16[1152,12,128]{2,1,0:T(8,128)(2,1)} reshape(bf16[3,3,128,1536]{3,2,1,0:T(8,128)(2,1)S(1)} %pad_maximum_fusion.2) | data formatting | bytes 7077888 | tf_op jit(solution)/shard_map/reshape | solution.py:37
  82.4 43.0 %collective-permute-done.7 = bf16[3,1,128,1536]{3,2,1,0:T(8,128)(2,1)} collective-permute-done((bf16[3,1,128,1536]{3,2,1,0:T(8,128)(2,1)}, bf16[3,1,128,1536]{3,2,1,0:T(8,128)(2,1)}, u32[]{:S(2)}, u32[]{:S(2)}) %collective-permute-start.7) | collective-permute-done | bytes 1179680 | tf_op jit(solution)/shard_map/ppermute | solution.py:24
  125.5 2.2 pad_maximum_fusion.3
  127.7 4.4 %reshape.163 = bf16[1152,12,128]{2,1,0:T(8,128)(2,1)} reshape(bf16[3,3,128,1536]{3,2,1,0:T(8,128)(2,1)S(1)} %pad_maximum_fusion.3) | data formatting | bytes 7077888 | tf_op jit(solution)/shard_map/reshape | solution.py:37
  132.1 6.5 %bitcast_select_fusion = f32[12,128,1152]{1,2,0:T(8,128)S(1)} fusion(bf16[12,128,128]{1,2,0:T(8,128)(2,1)} %bitcast.98, bf16[1152,12,128]{2,1,0:T(8,128)(2,1)} %reshape.162, f32[12,128]{1,0:T(8,128)S(1)} %bitcast.106, pred[12,1152]{1,0:T(8,128)(4,1)} %broadcast_and_fusion, pred[128]{0:T(512)(128)(4,1)} %iota_compare_fusion), kind=kOutput, calls=%fused_computation.5 | convolution fusion | flops 460062720 | bytes 11030144 | tf_op jit(solution)/shard_map/hrd,hcd->hrc/dot_general | solution.py:45
  138.5 2.8 convolution_convert_fusion
  141.4 0.2 copy-done.1
  141.6 1.8 fusion.1
  143.4 1.1 convolution_convert_fusion.1
  144.5 0.7 copy-done.2
  145.2 1.5 copy-done.4
  146.7 0.6 pad_maximum_fusion
  147.4 3.0 copy.67
  150.4 1.6 slice_bitcast_fusion.5
  152.0 26.6 %collective-permute-start.8 = (bf16[2,12,3,128,128]{4,3,1,0,2:T(8,128)(2,1)S(1)}, bf16[2,12,3,128,128]{4,3,1,0,2:T(8,128)(2,1)S(1)}, u32[]{:S(2)}, u32[]{:S(2)}) collective-permute-start(bf16[2,12,3,128,128]{4,3,1,0,2:T(8,128)(2,1)S(1)} %get-tuple-element.86), channel_id=1, source_target_pairs={{0,1},{1,2},{2,3},{3,4},{4,5},{5,6},{6,7},{8,9},{9,10},{10,11},{11... | collective-permute-start | bytes 7077896 | tf_op jit(solution)/shard_map/ppermute | solution.py:13
  178.6 1.5 collective-permute-start.9
  180.1 48.5 %collective-permute-done.8 = bf16[2,12,3,128,128]{4,3,1,0,2:T(8,128)(2,1)S(1)} collective-permute-done((bf16[2,12,3,128,128]{4,3,1,0,2:T(8,128)(2,1)S(1)}, bf16[2,12,3,128,128]{4,3,1,0,2:T(8,128)(2,1)S(1)}, u32[]{:S(2)}, u32[]{:S(2)}) %collective-permute-start.8) | collective-permute-done | bytes 2359328 | tf_op jit(solution)/shard_map/ppermute | solution.py:13
  228.6 54.4 %collective-permute-done.9 = bf16[2,12,3,128,128]{4,3,1,0,2:T(8,128)(2,1)S(1)} collective-permute-done((bf16[2,12,3,128,128]{4,3,1,0,2:T(8,128)(2,1)S(1)}, bf16[2,12,3,128,128]{4,3,1,0,2:T(8,128)(2,1)S(1)}, u32[]{:S(2)}, u32[]{:S(2)}) %collective-permute-start.9) | collective-permute-done | bytes 2359328 | tf_op jit(solution)/shard_map/ppermute | solution.py:13
  282.9 0.8 pad_maximum_fusion.1
  283.8 3.2 slice_bitcast_fusion.2
  287.0 2.3 copy-done
  289.3 5.6 %collective-permute-start.10 = (bf16[2,12,3,128,128]{4,3,1,0,2:T(8,128)(2,1)}, bf16[2,12,3,128,128]{4,3,1,0,2:T(8,128)(2,1)S(1)}, u32[]{:S(2)}, u32[]{:S(2)}) collective-permute-start(bf16[2,12,3,128,128]{4,3,1,0,2:T(8,128)(2,1)} %get-tuple-element.84), channel_id=1, source_target_pairs={{0,8},{8,16},{16,24},{1,9},{9,17},{17,25},{2,10},{10,18},{18,26},{... | collective-permute-start | bytes 7077896 | tf_op jit(solution)/shard_map/ppermute | solution.py:13
  294.9 1.3 collective-permute-start.11
  296.2 2.4 fusion.9
  298.6 0.9 copy.56
  299.5 44.8 %collective-permute-done.10 = bf16[2,12,3,128,128]{4,3,1,0,2:T(8,128)(2,1)S(1)} collective-permute-done((bf16[2,12,3,128,128]{4,3,1,0,2:T(8,128)(2,1)}, bf16[2,12,3,128,128]{4,3,1,0,2:T(8,128)(2,1)S(1)}, u32[]{:S(2)}, u32[]{:S(2)}) %collective-permute-start.10) | collective-permute-done | bytes 2359328 | tf_op jit(solution)/shard_map/ppermute | solution.py:13
  344.4 57.2 %collective-permute-done.11 = bf16[2,12,3,128,128]{4,3,1,0,2:T(8,128)(2,1)} collective-permute-done((bf16[2,12,3,128,128]{4,3,1,0,2:T(8,128)(2,1)}, bf16[2,12,3,128,128]{4,3,1,0,2:T(8,128)(2,1)}, u32[]{:S(2)}, u32[]{:S(2)}) %collective-permute-start.11) | collective-permute-done | bytes 2359328 | tf_op jit(solution)/shard_map/ppermute | solution.py:13
  401.6 3.4 add_reduce_fusion
  405.0 0.1 slice_bitcast_fusion.6
  405.1 0.2 copy.55
  405.3 0.9 copy.58
  406.2 0.2 copy.54
  406.5 0.9 copy.57
  (38 shorter events, 0.2 us)
Async XLA Ops:
  0.6 59.1 %copy-start.10 = (bf16[1,1,128,1536]{3,2,1,0:T(8,128)(2,1)S(1)}, bf16[1,1,128,1536]{3,2,1,0:T(8,128)(2,1)}, u32[]{:S(2)}) copy-start(bf16[1,1,128,1536]{3,2,1,0:T(8,128)(2,1)} %param.20) | copy-start | bytes 1179652
  0.6 60.0 %copy-start.11 = (bf16[1,1,128,1536]{3,2,1,0:T(8,128)(2,1)S(1)}, bf16[1,1,128,1536]{3,2,1,0:T(8,128)(2,1)}, u32[]{:S(2)}) copy-start(bf16[1,1,128,1536]{3,2,1,0:T(8,128)(2,1)} %param.23) | copy-start | bytes 1179652
  0.6 20.2 %collective-permute-start = (bf16[1,1,128,1536]{3,2,1,0:T(8,128)(2,1)}, bf16[1,1,128,1536]{3,2,1,0:T(8,128)(2,1)S(1)}, u32[]{:S(2)}, u32[]{:S(2)}) collective-permute-start(bf16[1,1,128,1536]{3,2,1,0:T(8,128)(2,1)} %param.21), channel_id=1, source_target_pairs={{0,8},{8,16},{16,24},{1,9},{9,17},{17,25},{2,10},{10,18},{18,26},{... | collective-permute-start | bytes 1179656 | tf_op jit(solution)/shard_map/ppermute | solution.py:21
  7.4 32.7 %collective-permute-start.1 = (bf16[1,1,128,1536]{3,2,1,0:T(8,128)(2,1)}, bf16[1,1,128,1536]{3,2,1,0:T(8,128)(2,1)S(1)}, u32[]{:S(2)}, u32[]{:S(2)}) collective-permute-start(bf16[1,1,128,1536]{3,2,1,0:T(8,128)(2,1)} %param.21), channel_id=1, source_target_pairs={{8,0},{16,8},{24,16},{9,1},{17,9},{25,17},{10,2},{18,10},{26,18},{... | collective-permute-start | bytes 1179656 | tf_op jit(solution)/shard_map/ppermute | solution.py:24
  8.7 37.8 %collective-permute-start.4 = (bf16[1,1,128,1536]{3,2,1,0:T(8,128)(2,1)}, bf16[1,1,128,1536]{3,2,1,0:T(8,128)(2,1)}, u32[]{:S(2)}, u32[]{:S(2)}) collective-permute-start(bf16[1,1,128,1536]{3,2,1,0:T(8,128)(2,1)} %param.22), channel_id=1, source_target_pairs={{0,8},{8,16},{16,24},{1,9},{9,17},{17,25},{2,10},{10,18},{18,26},{... | collective-permute-start | bytes 1179656 | tf_op jit(solution)/shard_map/ppermute | solution.py:21
  17.1 32.9 %collective-permute-start.5 = (bf16[1,1,128,1536]{3,2,1,0:T(8,128)(2,1)}, bf16[1,1,128,1536]{3,2,1,0:T(8,128)(2,1)S(1)}, u32[]{:S(2)}, u32[]{:S(2)}) collective-permute-start(bf16[1,1,128,1536]{3,2,1,0:T(8,128)(2,1)} %param.22), channel_id=1, source_target_pairs={{8,0},{16,8},{24,16},{9,1},{17,9},{25,17},{10,2},{18,10},{26,18},{... | collective-permute-start | bytes 1179656 | tf_op jit(solution)/shard_map/ppermute | solution.py:24
  19.3 39.1 %copy-start.13 = (f32[1,1,12,128]{3,1,2,0:T(1,128)S(1)}, f32[1,1,12,128]{3,1,2,0:T(1,128)}, u32[]{:S(2)}) copy-start(f32[1,1,12,128]{3,1,2,0:T(1,128)} %param.25) | copy-start | bytes 18436
  40.2 34.6 %copy-start.7 = (bf16[3,1,128,1536]{3,2,1,0:T(8,128)(2,1)}, bf16[3,1,128,1536]{3,2,1,0:T(8,128)(2,1)S(1)}, u32[]{:S(2)}) copy-start(bf16[3,1,128,1536]{3,2,1,0:T(8,128)(2,1)S(1)} %constant_dynamic-update-slice_fusion) | copy-start | bytes 3538948
  40.2 34.6 %collective-permute-start.3 = (bf16[3,1,128,1536]{3,2,1,0:T(8,128)(2,1)S(1)}, bf16[3,1,128,1536]{3,2,1,0:T(8,128)(2,1)S(1)}, u32[]{:S(2)}, u32[]{:S(2)}) collective-permute-start(bf16[3,1,128,1536]{3,2,1,0:T(8,128)(2,1)S(1)} %constant_dynamic-update-slice_fusion), channel_id=1, source_target_pairs={{1,0},{2,1},{3,2},{4,3},{5,4},{6,5},{7,6},{9,8},{10,9},{11,10},{12... | collective-permute-start | bytes 3538952 | tf_op jit(solution)/shard_map/ppermute | solution.py:24
  41.5 34.3 %collective-permute-start.2 = (bf16[3,1,128,1536]{3,2,1,0:T(8,128)(2,1)S(1)}, bf16[3,1,128,1536]{3,2,1,0:T(8,128)(2,1)}, u32[]{:S(2)}, u32[]{:S(2)}) collective-permute-start(bf16[3,1,128,1536]{3,2,1,0:T(8,128)(2,1)S(1)} %constant_dynamic-update-slice_fusion), channel_id=1, source_target_pairs={{0,1},{1,2},{2,3},{3,4},{4,5},{5,6},{6,7},{8,9},{9,10},{10,11},{11... | collective-permute-start | bytes 3538952 | tf_op jit(solution)/shard_map/ppermute | solution.py:21
  50.9 74.6 %collective-permute-start.7 = (bf16[3,1,128,1536]{3,2,1,0:T(8,128)(2,1)}, bf16[3,1,128,1536]{3,2,1,0:T(8,128)(2,1)}, u32[]{:S(2)}, u32[]{:S(2)}) collective-permute-start(bf16[3,1,128,1536]{3,2,1,0:T(8,128)(2,1)} %constant_dynamic-update-slice_fusion.3), channel_id=1, source_target_pairs={{1,0},{2,1},{3,2},{4,3},{5,4},{6,5},{7,6},{9,8},{10,9},{11,10},{12... | collective-permute-start | bytes 3538952 | tf_op jit(solution)/shard_map/ppermute | solution.py:24
  52.1 73.3 %collective-permute-start.6 = (bf16[3,1,128,1536]{3,2,1,0:T(8,128)(2,1)}, bf16[3,1,128,1536]{3,2,1,0:T(8,128)(2,1)}, u32[]{:S(2)}, u32[]{:S(2)}) collective-permute-start(bf16[3,1,128,1536]{3,2,1,0:T(8,128)(2,1)} %constant_dynamic-update-slice_fusion.3), channel_id=1, source_target_pairs={{0,1},{1,2},{2,3},{3,4},{4,5},{5,6},{6,7},{8,9},{9,10},{10,11},{11... | collective-permute-start | bytes 3538952 | tf_op jit(solution)/shard_map/ppermute | solution.py:21
  62.1 12.7 %copy-start.5 = (bf16[1,1,128,1536]{2,3,1,0:T(8,128)(2,1)}, bf16[1,1,128,1536]{2,3,1,0:T(8,128)(2,1)S(1)}, u32[]{:S(2)}) copy-start(bf16[1,1,128,1536]{2,3,1,0:T(8,128)(2,1)S(1)} %copy.43) | copy-start | bytes 1179652
  74.8 1.0 copy-start.9
  127.6 4.4 %copy-start.12 = (f32[1,1,12,128]{3,2,1,0:T(8,128)S(1)}, f32[1,1,12,128]{3,2,1,0:T(8,128)}, u32[]{:S(2)}) copy-start(f32[1,1,12,128]{3,2,1,0:T(8,128)} %copy.83) | copy-start | bytes 18436
  132.0 6.5 %copy-start.6 = (bf16[1,1,128,1536]{2,3,1,0:T(8,128)(2,1)S(1)}, bf16[1,1,128,1536]{2,3,1,0:T(8,128)(2,1)}, u32[]{:S(2)}) copy-start(bf16[1,1,128,1536]{2,3,1,0:T(8,128)(2,1)} %copy-done.5) | copy-start | bytes 1179652
  138.5 3.1 copy-start.1
  141.6 1.8 copy-start.8
  143.4 1.8 copy-start.2
  143.4 3.3 copy-start.4
  150.4 145.8 %slice-start = ((s8[4718592]{0:T(1024)(128)(4,1)}), s8[524288]{0:T(1024)(128)(4,1)S(1)}, s32[]{:S(2)}) async-start(s8[4718592]{0:T(1024)(128)(4,1)} %bitcast.93), calls=%async_computation | async-start | bytes 1048576
  152.0 76.6 %collective-permute-start.8 = (bf16[2,12,3,128,128]{4,3,1,0,2:T(8,128)(2,1)S(1)}, bf16[2,12,3,128,128]{4,3,1,0,2:T(8,128)(2,1)S(1)}, u32[]{:S(2)}, u32[]{:S(2)}) collective-permute-start(bf16[2,12,3,128,128]{4,3,1,0,2:T(8,128)(2,1)S(1)} %get-tuple-element.86), channel_id=1, source_target_pairs={{0,1},{1,2},{2,3},{3,4},{4,5},{5,6},{6,7},{8,9},{9,10},{10,11},{11... | collective-permute-start | bytes 7077896 | tf_op jit(solution)/shard_map/ppermute | solution.py:13
  178.6 104.3 %collective-permute-start.9 = (bf16[2,12,3,128,128]{4,3,1,0,2:T(8,128)(2,1)S(1)}, bf16[2,12,3,128,128]{4,3,1,0,2:T(8,128)(2,1)S(1)}, u32[]{:S(2)}, u32[]{:S(2)}) collective-permute-start(bf16[2,12,3,128,128]{4,3,1,0,2:T(8,128)(2,1)S(1)} %get-tuple-element.87), channel_id=1, source_target_pairs={{1,0},{2,1},{3,2},{4,3},{5,4},{6,5},{7,6},{9,8},{10,9},{11,10},{12... | collective-permute-start | bytes 7077896 | tf_op jit(solution)/shard_map/ppermute | solution.py:13
  282.9 13.3 %slice-start.1 = ((s8[4718592]{0:T(1024)(128)(4,1)}), s8[4194304]{0:T(1024)(128)(4,1)S(1)}, s32[]{:S(2)}) async-start(s8[4718592]{0:T(1024)(128)(4,1)} %bitcast.93), calls=%async_computation.1 | async-start | bytes 8388608
  283.8 5.5 %copy-start = (bf16[2,12,3,3,128,128]{5,4,1,0,3,2:T(8,128)(2,1)}, bf16[2,12,3,3,128,128]{5,4,1,0,3,2:T(8,128)(2,1)S(1)}, u32[]{:S(2)}) copy-start(bf16[2,12,3,3,128,128]{5,4,1,0,3,2:T(8,128)(2,1)S(1)} %pad_maximum_fusion.1) | copy-start | bytes 21233668
  283.8 12.5 %copy-start.3 = (bf16[12,128,1152]{1,2,0:T(8,128)(2,1)S(1)}, bf16[12,128,1152]{1,2,0:T(8,128)(2,1)}, u32[]{:S(2)}) copy-start(bf16[12,128,1152]{1,2,0:T(8,128)(2,1)} %copy-done.2) | copy-start | bytes 10616836
  289.3 55.1 %collective-permute-start.10 = (bf16[2,12,3,128,128]{4,3,1,0,2:T(8,128)(2,1)}, bf16[2,12,3,128,128]{4,3,1,0,2:T(8,128)(2,1)S(1)}, u32[]{:S(2)}, u32[]{:S(2)}) collective-permute-start(bf16[2,12,3,128,128]{4,3,1,0,2:T(8,128)(2,1)} %get-tuple-element.84), channel_id=1, source_target_pairs={{0,8},{8,16},{16,24},{1,9},{9,17},{17,25},{2,10},{10,18},{18,26},{... | collective-permute-start | bytes 7077896 | tf_op jit(solution)/shard_map/ppermute | solution.py:13
  294.9 106.7 %collective-permute-start.11 = (bf16[2,12,3,128,128]{4,3,1,0,2:T(8,128)(2,1)}, bf16[2,12,3,128,128]{4,3,1,0,2:T(8,128)(2,1)}, u32[]{:S(2)}, u32[]{:S(2)}) collective-permute-start(bf16[2,12,3,128,128]{4,3,1,0,2:T(8,128)(2,1)} %get-tuple-element.85), channel_id=1, source_target_pairs={{8,0},{16,8},{24,16},{9,1},{17,9},{25,17},{10,2},{18,10},{26,18},{... | collective-permute-start | bytes 7077896 | tf_op jit(solution)/shard_map/ppermute | solution.py:13
where the time goes:
time: 408 us; the launch traced here: 407 us
  waiting for transfers between devices  277 us (68%)
  starting transfers between devices  65.4 us (16%)
  local copies, waits for them, and re-layouts  37.1 us (9%)
  matrix products  14.5 us (4%)
  other arithmetic  12 us (3%)
    ppermute x4, waiting for transfers between devices, passed_along(): return lax.ppermute(block, axis, route)  205 us
    ppermute x4, waiting for transfers between devices, with_halo(): lax.ppermute(lax.slice_in_dim(block, 0, width, axis=dim), axis, backward)  72.5 us
    ppermute x4, starting transfers between devices, passed_along(): return lax.ppermute(block, axis, route)  35 us
    ppermute x4, starting transfers between devices, with_halo(): lax.ppermute(lax.slice_in_dim(block, block.shape[dim] - width, None, axis...  25.2 us
    unnamed x45, local copies, waits for them, and re-layouts  16.7 us
    reshape x2, local copies, waits for them, and re-layouts, heads_first(): return jnp.transpose(tiles.reshape(-1, HEADS, HEAD_DIM), (1, 0, 2))  8.78 us
  transfers between devices with their start and end apart: 12, of which 7 were waited for; matrix products, arithmetic and copies ran while one was open for 6% of the time, Pallas kernels for 0%

commit v1 on v0

v1 whole, which is shorter than its diff:
```python
import functools
import math

import jax
import jax.numpy as jnp
from jax import lax
from jax.experimental import pallas as pl
from jax.experimental.pallas import tpu as pltpu
from jax.sharding import PartitionSpec as P

HEADS = 12
HEAD_DIM = 128
TOK = 128
TILES_T = 4
TILES_H = 8
MESH = pl.DeviceIdType.MESH
FAR = 1e30
LOG2E = math.log2(math.e)
SCALE = HEAD_DIM ** (-0.5)

ROW_Q, ROW_G, ROW_S, ROWS = 0, 128, 256, 272

VARIANTS = (
    (12, 0, 0), (7, 2, 2), (6, 2, 3), (5, 2, 3), (4, 2, 3), (3, 2, 3), (4, 1, 4), (4, 4, 1),
)

OFFSETS = ((0, 1), (-1, 0), (1, 1), (-1, 1), (1, 0), (0, -1), (1, -1), (-1, -1))
TERM = {6: 0, 5: 1, 7: 2, 4: 3, 2: 4, 1: 5, 0: 6, 3: 7}


def nt(a, b):
    return lax.dot_general(a, b, (((1,), (1,)), ((), ())), preferred_element_type=jnp.float32)


def nn(a, b):
    return jnp.dot(a, b, preferred_element_type=jnp.float32)


def tn(a, b):
    return lax.dot_general(a, b, (((0,), (0,)), ((), ())), preferred_element_type=jnp.float32)


def split3(x):
    hi = x.astype(jnp.bfloat16)
    rest = x - hi.astype(jnp.float32)
    mid = rest.astype(jnp.bfloat16)
    lo = (rest - mid.astype(jnp.float32)).astype(jnp.bfloat16)
    return [hi, mid, lo]


def loop(low, high, body):
    if high > low:
        lax.fori_loop(low, high, lambda i, c: (body(i), c)[1], 0)


def kernel(
    counts_abc,
    own, kv, pen, res,
    rcv11, rcv10, rcv01, out11, in11, out10, in10, out01, in01, held,
    ss11, rs11, ss10, rs10, ss01, rs01,
):
    A, B, C = counts_abc
    grp, ta, ha = lax.axis_index("grp"), lax.axis_index("ta"), lax.axis_index("ha")
    x, p = ha // 2, lax.rem(ha, 2)
    z = ta * 2 + p
    s = 1 - 2 * p

    def dev(dx, dz):
        zz = lax.rem(z + dz * s + 8, 8)
        xx = lax.rem(x + dx * s + 4, 4)
        return (grp, zz // 2, xx * 2 + lax.rem(zz, 2))

    zf, zb, xf, xb, z2f, z2b = dev(0, 1), dev(0, -1), dev(1, 0), dev(-1, 0), dev(0, 2), dev(0, -2)

    barrier = pltpu.get_barrier_semaphore()
    for d in (zf, zb, xf, xb, z2f, z2b):
        pl.semaphore_signal(barrier, inc=1, device_id=d, device_id_type=MESH)

    def remote(src, dst, ssem, rsem, to):
        return pltpu.make_async_remote_copy(
            src_ref=src, dst_ref=dst, send_sem=ssem, recv_sem=rsem, device_id=to, device_id_type=MESH
        )

    def copy11(e, t):
        src = (
            own.at[t], rcv11.at[t, 0], rcv11.at[t, 1], own.at[t],
            rcv11.at[t, 3], rcv11.at[t, 0], rcv11.at[t, 2], rcv11.at[t, 3],
        )[e]
        to = (zf, zb, zf, zb, zf, xf, xf, xf)[e]
        return remote(src, rcv11.at[t, e], ss11.at[t, e], rs11.at[t, e], to)

    def back11(i, t):
        if i == 0:
            return remote(out11.at[t, pl.ds(0, 3)], in11.at[t, pl.ds(0, 3)], ss11.at[t, 8], rs11.at[t, 8], xb)
        to = {3: zf, 4: zf, 5: zb, 6: zf, 7: zb}[i]
        return remote(out11.at[t, i], in11.at[t, i], ss11.at[t, 6 + i], rs11.at[t, 6 + i], to)

    def copy10(e, t):
        return remote(own.at[A + t], rcv10.at[t, e], ss10.at[t, e], rs10.at[t, e], (z2f, z2b)[e])

    def back10(e, t):
        return remote(out10.at[t, e], in10.at[t, e], ss10.at[t, 2 + e], rs10.at[t, 2 + e], (z2b, z2f)[e])

    def copy01(e, t):
        src = own.at[A + B + t] if e == 0 else rcv01.at[t, 0]
        return remote(src, rcv01.at[t, e], ss01.at[t, e], rs01.at[t, e], (zf, xf)[e])

    def back01(e, t):
        return remote(out01.at[t, e], in01.at[t, e], ss01.at[t, 2 + e], rs01.at[t, 2 + e], (zf, xb)[e])

    def compute(j, blocks):
        k0, v0 = kv[j, 0], kv[j, 1]
        lse_rows, delta_rows = [], []
        for ref, e in blocks:
            rows = ref[ROW_S:ROW_S + 16].astype(jnp.float32)
            lse_row = rows[0:1] + rows[1:2] + rows[2:3]
            lse_rows.append(lse_row if e is None else lse_row + pen[j, e:e + 1])
            delta_rows.append(rows[3:4] + rows[4:5] + rows[5:6])
        qs = jnp.concatenate([ref[ROW_Q:ROW_Q + TOK] for ref, _ in blocks], axis=0)
        gs = jnp.concatenate([ref[ROW_G:ROW_G + TOK] for ref, _ in blocks], axis=0)
        lse_row, delta_row = jnp.concatenate(lse_rows, axis=1), jnp.concatenate(delta_rows, axis=1)
        prob = jnp.exp2(nt(k0, qs) * (SCALE * LOG2E) - lse_row)
        ds = (prob * (nt(v0, gs) - delta_row) * SCALE).astype(jnp.bfloat16)
        res[j, 2] = nn(prob.astype(jnp.bfloat16), gs).astype(jnp.bfloat16)
        res[j, 1] = nn(ds, qs).astype(jnp.bfloat16)
        dq = tn(ds, k0)
        return [dq[i * TOK:(i + 1) * TOK] for i in range(len(blocks))]

    def f32(v):
        return v.astype(jnp.float32)

    def attend11(t):
        blocks = [(own.at[t], None)] + [(rcv11.at[t, e], e) for e in range(8)]
        parts = compute(t, blocks)
        for e in range(8):
            if TERM[e] < 4:
                out11[t, TERM[e]] = parts[1 + e].astype(jnp.bfloat16)
            else:
                held[t, TERM[e] - 4] = parts[1 + e]
        held[t, 4] = parts[0]

    pl.semaphore_wait(barrier, 6)

    def start11(t):
        copy11(0, t).start()
        copy11(3, t).start()

    loop(0, A, start11)

    def others_out():
        def start10(t):
            copy10(0, t).start()
            copy10(1, t).start()

        loop(0, B, start10)
        loop(0, C, lambda t: copy01(0, t).start())

    def plain(j):
        res[j, 0] = compute(j, [(own.at[j], None)])[0].astype(jnp.bfloat16)

    def relay01(t):
        copy01(0, t).wait_recv()
        copy01(1, t).start()

    def attend10(t):
        copy10(0, t).wait_recv()
        copy10(1, t).wait_recv()
        j = A + t
        parts = compute(j, [(own.at[j], None), (rcv10.at[t, 0], 1), (rcv10.at[t, 1], 4)])
        held[j, 4] = parts[0]
        for e in range(2):
            out10[t, e] = parts[1 + e].astype(jnp.bfloat16)
            back10(e, t).start()

    def attend01(t):
        copy01(1, t).wait_recv()
        j = A + B + t
        parts = compute(j, [(own.at[j], None), (rcv01.at[t, 0], 0), (rcv01.at[t, 1], 5)])
        held[j, 4] = parts[0]
        held[j, 2] = parts[1]
        out01[t, 1] = parts[2].astype(jnp.bfloat16)
        back01(1, t).start()

    def merge01(t):
        back01(1, t).wait_recv()
        out01[t, 0] = (held[A + B + t, 2] + f32(in01[t, 1])).astype(jnp.bfloat16)
        back01(0, t).start()

    def step(t):
        @pl.when(t < A)
        def _():
            copy11(0, t).wait_recv()
            copy11(1, t).start()
            copy11(5, t).start()
            copy11(3, t).wait_recv()
            copy11(4, t).start()
            copy11(7, t).start()

        @pl.when(t == 0)
        def _():
            others_out()

        @pl.when((t >= 1) & (t < A + 1))
        def _():
            copy11(1, t - 1).wait_recv()
            copy11(2, t - 1).start()

        @pl.when((t >= 2) & (t < A + 2))
        def _():
            copy11(2, t - 2).wait_recv()
            copy11(6, t - 2).start()

        @pl.when(t == 2)
        def _():
            loop(0, C, relay01)
            loop(A + B + C, HEADS, plain)

        @pl.when((t >= 3) & (t < A + 3))
        def _():
            u = t - 3
            for e in (4, 5, 7, 6):
                copy11(e, u).wait_recv()
            attend11(u)
            back11(0, u).start()
            back11(3, u).start()

        @pl.when(t == 3)
        def _():
            loop(0, B, attend10)
            loop(0, C, attend01)

        @pl.when((t >= 4) & (t < A + 4))
        def _():
            u = t - 4
            back11(0, u).wait_recv()
            out11[u, 4] = (held[u, 0] + f32(in11[u, 0])).astype(jnp.bfloat16)
            back11(4, u).start()
            back11(3, u).wait_recv()
            out11[u, 7] = (held[u, 3] + f32(in11[u, 2]) + f32(in11[u, 3])).astype(jnp.bfloat16)
            back11(7, u).start()

        @pl.when(t == 4)
        def _():
            loop(0, C, merge01)

        @pl.when((t >= 5) & (t < A + 5))
        def _():
            u = t - 5
            back11(4, u).wait_recv()
            out11[u, 5] = (held[u, 1] + f32(in11[u, 4])).astype(jnp.bfloat16)
            back11(5, u).start()

        @pl.when((t >= 6) & (t < A + 6))
        def _():
            u = t - 6
            back11(5, u).wait_recv()
            out11[u, 6] = (held[u, 2] + f32(in11[u, 1]) + f32(in11[u, 5])).astype(jnp.bfloat16)
            back11(6, u).start()

        @pl.when(t >= 7)
        def _():
            u = t - 7
            back11(7, u).wait_recv()
            back11(6, u).wait_recv()
            res[u, 0] = (held[u, 4] + f32(in11[u, 6]) + f32(in11[u, 7])).astype(jnp.bfloat16)

    loop(0, A + 7, step)

    def finish10(t):
        back10(0, t).wait_recv()
        back10(1, t).wait_recv()
        j = A + t
        res[j, 0] = (held[j, 4] + f32(in10[t, 0]) + f32(in10[t, 1])).astype(jnp.bfloat16)

    def finish01(t):
        back01(0, t).wait_recv()
        j = A + B + t
        res[j, 0] = (held[j, 4] + f32(in01[t, 0])).astype(jnp.bfloat16)

    loop(0, B, finish10)
    loop(0, C, finish01)

    def drain11(t):
        for e in range(8):
            copy11(e, t).wait_send()
        for i in (0, 3, 4, 5, 6, 7):
            back11(i, t).wait_send()

    def drain10(t):
        for e in range(2):
            copy10(e, t).wait_send()
            back10(e, t).wait_send()

    def drain01(t):
        for e in range(2):
            copy01(e, t).wait_send()
            back01(e, t).wait_send()

    loop(0, A, drain11)
    loop(0, B, drain10)
    loop(0, C, drain01)


def ordered(
    reach_ref, counts_ref, q_ref, k_ref, v_ref, o_ref, g_ref, lse_ref,
    choice_ref, slot_ref, own, kv, pen, perm_ref,
):
    ta, ha = lax.axis_index("ta"), lax.axis_index("ha")
    s = 1 - 2 * lax.rem(ha, 2)
    live = counts_ref[ta, ha]
    rt = [reach_ref[h, 0] for h in range(HEADS)]
    rh = [reach_ref[h, 1] for h in range(HEADS)]
    n11 = sum(t * h for t, h in zip(rt, rh))
    n10 = sum(rt) - n11
    n01 = sum(rh) - n11
    choice, A, B, C = [jnp.int32(v) for v in (0, *VARIANTS[0])]
    for i in sorted(range(len(VARIANTS)), key=lambda i: -price(VARIANTS[i])):
        a, b, c = VARIANTS[i]
        fits = n11 + jnp.maximum(n10 - b, 0) + jnp.maximum(n01 - c, 0) <= a
        choice, A, B, C = [jnp.where(fits, new, old) for new, old in zip((i, a, b, c), (choice, A, B, C))]
    choice_ref[0] = choice
    c11, c10, c01, c00 = [jnp.int32(0)] * 4
    first = []
    for h in range(HEADS):
        own10 = (rt[h] == 1) & (rh[h] == 0) & (c10 < B)
        own01 = (rt[h] == 0) & (rh[h] == 1) & (c01 < C)
        none = (rt[h] == 0) & (rh[h] == 0)
        first.append(jnp.where(none, -1, jnp.where(own10, A + c10, jnp.where(own01, A + B + c01, c11))))
        c10 = c10 + jnp.where(own10, 1, 0)
        c01 = c01 + jnp.where(own01, 1, 0)
        c11 = c11 + jnp.where(own10 | own01 | none, 0, 1)
    for h in range(HEADS):
        none = first[h] < 0
        in11 = none & (c11 < A)
        in10 = none & (c11 >= A) & (c10 < B)
        in01 = none & (c11 >= A) & (c10 >= B) & (c01 < C)
        in00 = none & (c11 >= A) & (c10 >= B) & (c01 >= C)
        slot = jnp.where(
            none,
            jnp.where(in11, c11, jnp.where(in10, A + c10, jnp.where(in01, A + B + c01, A + B + C + c00))),
            first[h],
        )
        c11, c10, c01, c00 = [
            n + jnp.where(taken, 1, 0) for n, taken in ((c11, in11), (c10, in10), (c01, in01), (c00, in00))
        ]
        slot_ref[h] = slot
        perm_ref[slot] = h
    keep = lax.broadcasted_iota(jnp.int32, (TOK, HEAD_DIM), 0) < live
    lane_ids = lax.broadcasted_iota(jnp.int32, (1, TOK), 1)
    sub_ids = lax.broadcasted_iota(jnp.int32, (8, TOK), 0)
    for j in range(HEADS):
        h = perm_ref[j]
        c = pl.ds(pl.multiple_of(h * HEAD_DIM, HEAD_DIM), HEAD_DIM)
        g = g_ref[0, 0, :, c]
        own[j, ROW_Q:ROW_Q + TOK] = q_ref[0, 0, :, c]
        own[j, ROW_G:ROW_G + TOK] = g
        kv[j, 0] = jnp.where(keep, k_ref[0, 0, :, c].astype(jnp.float32), 0.0).astype(jnp.bfloat16)
        kv[j, 1] = v_ref[0, 0, :, c]
        prod = g.astype(jnp.float32) * o_ref[0, 0, :, c].astype(jnp.float32)
        delta_row = jnp.sum(prod.T, axis=0, keepdims=True)
        lse_row = lse_ref[0, 0, pl.ds(h, 1), :] * LOG2E
        rows = split3(jnp.where(lane_ids < live, lse_row, FAR)) + split3(delta_row)
        rows = [r.astype(jnp.float32) for r in rows] + [jnp.zeros((10, TOK), jnp.float32)]
        own[j, ROW_S:ROW_S + 16] = jnp.concatenate(rows, axis=0).astype(jnp.bfloat16)
        far = jnp.zeros((8, TOK), jnp.float32)
        for e, (dt, dh) in enumerate(OFFSETS):
            at, ah = ta + dt * s, ha + dh * s
            inside = (at >= 0) & (at < TILES_T) & (ah >= 0) & (ah < TILES_H)
            seen = inside & (reach_ref[h, 0] >= abs(dt)) & (reach_ref[h, 1] >= abs(dh))
            far = jnp.where(sub_ids == e, jnp.where(seen, jnp.float32(0.0), jnp.float32(FAR)), far)
        pen[j] = far


def restored(slot_ref, counts_ref, res, dq_ref, dk_ref, dv_ref):
    live = counts_ref[lax.axis_index("ta"), lax.axis_index("ha")]
    keep = lax.broadcasted_iota(jnp.int32, (TOK, HEAD_DIM), 0) < live
    for h in range(HEADS):
        j = slot_ref[h]
        c = slice(h * HEAD_DIM, (h + 1) * HEAD_DIM)
        dq_ref[0, 0, :, c] = res[j, 0]
        for i, out in ((1, dk_ref), (2, dv_ref)):
            out[0, 0, :, c] = jnp.where(keep, res[j, i].astype(jnp.float32), 0.0).astype(jnp.bfloat16)


def price(variant):
    A, B, C = variant
    return 9 * A + 6 * B + 3 * C


VMEM, SMEM = pl.BlockSpec(memory_space=pltpu.VMEM), pl.BlockSpec(memory_space=pltpu.SMEM)
OWN = (HEADS, ROWS, HEAD_DIM)


def exchange(index, own, kv, pen):
    A, B, C = VARIANTS[index]
    dma = pltpu.SemaphoreType.DMA
    b, c = max(B, 1), max(C, 1)
    return pl.pallas_call(
        functools.partial(kernel, (A, B, C)),
        out_shape=jax.ShapeDtypeStruct((HEADS, 3, TOK, HEAD_DIM), jnp.bfloat16),
        in_specs=[VMEM] * 3,
        out_specs=VMEM,
        scratch_shapes=[
            pltpu.VMEM((A, 8, ROWS, HEAD_DIM), jnp.bfloat16),
            pltpu.VMEM((b, 2, ROWS, HEAD_DIM), jnp.bfloat16),
            pltpu.VMEM((c, 2, ROWS, HEAD_DIM), jnp.bfloat16),
            pltpu.VMEM((A, 8, TOK, HEAD_DIM), jnp.bfloat16),
            pltpu.VMEM((A, 8, TOK, HEAD_DIM), jnp.bfloat16),
            pltpu.VMEM((b, 2, TOK, HEAD_DIM), jnp.bfloat16),
            pltpu.VMEM((b, 2, TOK, HEAD_DIM), jnp.bfloat16),
            pltpu.VMEM((c, 2, TOK, HEAD_DIM), jnp.bfloat16),
            pltpu.VMEM((c, 2, TOK, HEAD_DIM), jnp.bfloat16),
            pltpu.VMEM((HEADS, 5, TOK, HEAD_DIM), jnp.float32),
            dma((A, 14)), dma((A, 14)), dma((b, 4)), dma((b, 4)), dma((c, 4)), dma((c, 4)),
        ],
        compiler_params=pltpu.CompilerParams(
            collective_id=index, has_side_effects=True, vmem_limit_bytes=56 * 2**20
        ),
        name=f"exchange_{A}_{B}_{C}",
    )(own, kv, pen)


def per_device(queries, key_tiles, value_tiles, outputs, grads_out, log_sums, tile_counts, head_reach):
    params = pltpu.CompilerParams(vmem_limit_bytes=32 * 2**20)
    choice, slots, own, kv, pen = pl.pallas_call(
        ordered,
        out_shape=(
            jax.ShapeDtypeStruct((1,), jnp.int32),
            jax.ShapeDtypeStruct((HEADS,), jnp.int32),
            jax.ShapeDtypeStruct(OWN, jnp.bfloat16),
            jax.ShapeDtypeStruct((HEADS, 2, TOK, HEAD_DIM), jnp.bfloat16),
            jax.ShapeDtypeStruct((HEADS, 8, TOK), jnp.float32),
        ),
        in_specs=[SMEM] * 2 + [VMEM] * 6,
        out_specs=(SMEM, SMEM, VMEM, VMEM, VMEM),
        scratch_shapes=[pltpu.SMEM((HEADS,), jnp.int32)],
        compiler_params=params,
        name="ordered",
    )(head_reach, tile_counts, queries, key_tiles, value_tiles, outputs, grads_out, log_sums)
    branches = [functools.partial(exchange, i) for i in range(len(VARIANTS))]
    res = branches[0](own, kv, pen) if len(branches) == 1 else lax.switch(choice[0], branches, own, kv, pen)
    tile = jax.ShapeDtypeStruct((1, 1, TOK, HEADS * HEAD_DIM), jnp.bfloat16)
    return pl.pallas_call(
        restored,
        out_shape=(tile, tile, tile),
        in_specs=[SMEM, SMEM, VMEM],
        out_specs=(VMEM, VMEM, VMEM),
        compiler_params=params,
        name="restored",
    )(slots, tile_counts, res)


def solution(mesh):
    tiles = P(("grp", "ta"), "ha", None, None)
    return jax.shard_map(
        per_device, mesh=mesh,
        in_specs=(tiles,) * 6 + (P("grp", None), P()),
        out_specs=(tiles,) * 3, check_vma=False,
    )
```

time: 408 us -> 70.4 us (0.17)
  the two profiles are of different devices: /device:TPU:1 before, /device:TPU:8 now
where the time goes in v1:
time: 70.4 us; the launch traced here: 70 us
  Pallas kernels  61.1 us (87%)
  local copies, waits for them, and re-layouts  7.12 us (10%)
  between operations  1.32 us (2%)
    pallas_call x1, Pallas kernels, exchange(): pl.pallas_call(functools.partial(kernel, (A, B, C)), out_shape=jax.ShapeD...  57.3 us
    unnamed x16, local copies, waits for them, and re-layouts  7.12 us
    pallas_call x1, Pallas kernels, per_device(): pl.pallas_call(ordered, out_shape=(jax.ShapeDtypeStruct((1,), jnp.int32),...  2.04 us
    pallas_call x1, Pallas kernels, per_device(): pl.pallas_call(restored, out_shape=(tile, tile, tile), in_specs=[SMEM, SM...  1.73 us

profile of v1, /device:TPU:8, one launch (start us, length us, event | category | flops | bytes accessed | tf_op | source)
XLA Modules:
  0.0 70.0 jit_solution(4704025433189779539)
XLA Ops:
  0.6 0.7 copy.12.lse_ref
  1.3 0.8 %copy.11.reach_ref = s32[12,2]{1,0:T(8,128)S(1)} copy(s32[12,2]{0,1:T(2,128)} %param.23) | data formatting | bytes 192 | tf_op args[7]
  2.1 0.0 copy-start
  2.1 1.0 %copy-done = bf16[1,1,128,1536]{3,2,1,0:T(8,128)(2,1)S(1)} copy-done((bf16[1,1,128,1536]{3,2,1,0:T(8,128)(2,1)S(1)}, bf16[1,1,128,1536]{3,2,1,0:T(8,128)(2,1)}, u32[]{:S(2)}) %copy-start) | copy-done | bytes 393240
  3.1 0.0 copy-start.1
  3.1 1.0 %copy-done.1 = bf16[1,1,128,1536]{3,2,1,0:T(8,128)(2,1)S(1)} copy-done((bf16[1,1,128,1536]{3,2,1,0:T(8,128)(2,1)S(1)}, bf16[1,1,128,1536]{3,2,1,0:T(8,128)(2,1)}, u32[]{:S(2)}) %copy-start.1) | copy-done | bytes 393240
  4.1 0.0 copy-start.2
  4.1 1.0 %copy-done.2 = bf16[1,1,128,1536]{3,2,1,0:T(8,128)(2,1)S(1)} copy-done((bf16[1,1,128,1536]{3,2,1,0:T(8,128)(2,1)S(1)}, bf16[1,1,128,1536]{3,2,1,0:T(8,128)(2,1)}, u32[]{:S(2)}) %copy-start.2) | copy-done | bytes 393240
  5.1 0.0 copy-start.3
  5.1 1.0 %copy-done.3 = bf16[1,1,128,1536]{3,2,1,0:T(8,128)(2,1)S(1)} copy-done((bf16[1,1,128,1536]{3,2,1,0:T(8,128)(2,1)S(1)}, bf16[1,1,128,1536]{3,2,1,0:T(8,128)(2,1)}, u32[]{:S(2)}) %copy-start.3) | copy-done | bytes 393240
  6.1 0.0 copy-start.4
  6.1 1.0 %copy-done.4 = bf16[1,1,128,1536]{3,2,1,0:T(8,128)(2,1)S(1)} copy-done((bf16[1,1,128,1536]{3,2,1,0:T(8,128)(2,1)S(1)}, bf16[1,1,128,1536]{3,2,1,0:T(8,128)(2,1)}, u32[]{:S(2)}) %copy-start.4) | copy-done | bytes 393240
  7.1 0.0 copy-start.5
  7.1 0.7 copy-done.5
  7.8 2.0 %ordered.1 = (s32[1]{0:T(128)}, s32[12]{0:T(128)S(1)}, bf16[12,272,128]{2,1,0:T(8,128)(2,1)S(1)}, bf16[12,2,128,128]{3,2,1,0:T(8,128)(2,1)S(1)}, f32[12,8,128]{2,1,0:T(8,128)S(1)}) custom-call(s32[12,2]{1,0:T(8,128)S(1)} %copy.11.reach_ref, s32[4,8]{1,0:T(4,128)S(1)} %copy-done.5, bf16[1,1,128,1536]{3,2,1,0:T(8,128)(2,1)S(1)} %copy-done, ...), custom_call_target="tpu_custom_call" | custom-call | tf_op jit(solution)/shard_map/ordered/pallas_call | solution.py:425
  10.5 0.0 copy-start.6
  10.5 57.7 %conditional.1 = (bf16[12,3,128,128]{3,2,1,0:T(8,128)(2,1)S(1)}) conditional(s32[]{:T(128)} %bitcast, (bf16[12,272,128]{2,1,0:T(8,128)(2,1)S(1)}, bf16[12,2,128,128]{3,2,1,0:T(8,128)(2,1)S(1)}, f32[12,8,128]{2,1,0:T(8,128)S(1)}) %tuple.31, (bf16[12,272,128]{2,1,0:T(8,128)(2,1)S(1)}, ...), branch_computations={%region_0.0_spmd, %region_1.0_spmd, %region_2.0_spmd, %region_3.0_... | conditional | bytes 8 | solution.py:441
  10.5 57.3 %exchange_3_2_3.1 = bf16[12,3,128,128]{3,2,1,0:T(8,128)(2,1)S(1)} custom-call(bf16[12,272,128]{2,1,0:T(8,128)(2,1)S(1)} %get-tuple-element.72.own, bf16[12,2,128,128]{3,2,1,0:T(8,128)(2,1)S(1)} %get-tuple-element.73.kv, f32[12,8,128]{2,1,0:T(8,128)S(1)} %get-tuple-element.74.pen), custom_call_target="tpu_custom_call" | custom-call | tf_op jit(solution)/shard_map/cond/branch_5_fun/exchange_3_2_3/pallas_call | solution.py:398
  68.2 0.0 copy-done.6
  68.2 1.7 %restored.1 = (bf16[1,1,128,1536]{3,2,1,0:T(8,128)(2,1)}, bf16[1,1,128,1536]{3,2,1,0:T(8,128)(2,1)}, bf16[1,1,128,1536]{3,2,1,0:T(8,128)(2,1)}) custom-call(s32[12]{0:T(128)S(1)} %get-tuple-element.89.slot_ref, s32[4,8]{1,0:T(4,128)S(1)} %copy-done.6, bf16[12,3,128,128]{3,2,1,0:T(8,128)(2,1)S(1)} %get-tuple-element.94.res), custom_call_target="tpu_custom_call" | custom-call | tf_op jit(solution)/shard_map/restored/pallas_call | solution.py:443
Async XLA Ops:
  2.1 1.0 %copy-start = (bf16[1,1,128,1536]{3,2,1,0:T(8,128)(2,1)S(1)}, bf16[1,1,128,1536]{3,2,1,0:T(8,128)(2,1)}, u32[]{:S(2)}) copy-start(bf16[1,1,128,1536]{3,2,1,0:T(8,128)(2,1)} %q_ref.1) | copy-start | bytes 1179652
  3.1 1.0 %copy-start.1 = (bf16[1,1,128,1536]{3,2,1,0:T(8,128)(2,1)S(1)}, bf16[1,1,128,1536]{3,2,1,0:T(8,128)(2,1)}, u32[]{:S(2)}) copy-start(bf16[1,1,128,1536]{3,2,1,0:T(8,128)(2,1)} %k_ref.1) | copy-start | bytes 1179652
  4.1 1.0 %copy-start.2 = (bf16[1,1,128,1536]{3,2,1,0:T(8,128)(2,1)S(1)}, bf16[1,1,128,1536]{3,2,1,0:T(8,128)(2,1)}, u32[]{:S(2)}) copy-start(bf16[1,1,128,1536]{3,2,1,0:T(8,128)(2,1)} %v_ref.1) | copy-start | bytes 1179652
  5.1 1.0 %copy-start.3 = (bf16[1,1,128,1536]{3,2,1,0:T(8,128)(2,1)S(1)}, bf16[1,1,128,1536]{3,2,1,0:T(8,128)(2,1)}, u32[]{:S(2)}) copy-start(bf16[1,1,128,1536]{3,2,1,0:T(8,128)(2,1)} %o_ref.1) | copy-start | bytes 1179652
  6.1 1.0 %copy-start.4 = (bf16[1,1,128,1536]{3,2,1,0:T(8,128)(2,1)S(1)}, bf16[1,1,128,1536]{3,2,1,0:T(8,128)(2,1)}, u32[]{:S(2)}) copy-start(bf16[1,1,128,1536]{3,2,1,0:T(8,128)(2,1)} %g_ref.1) | copy-start | bytes 1179652
  7.1 0.7 copy-start.5
  10.5 57.8 %copy-start.6 = (s32[4,8]{1,0:T(4,128)S(1)}, s32[4,8]{1,0:T(4,128)}, u32[]{:S(2)}) copy-start(s32[4,8]{1,0:T(4,128)} %counts_ref.3) | copy-start | bytes 388

commit v2 on v1

--- a/solution.py
+++ b/solution.py
@@ -21,7 +21,8 @@
 ROW_Q, ROW_G, ROW_S, ROWS = 0, 128, 256, 272
 
 VARIANTS = (
-    (12, 0, 0), (7, 2, 2), (6, 2, 3), (5, 2, 3), (4, 2, 3), (3, 2, 3), (4, 1, 4), (4, 4, 1),
+    (12, 0, 0), (9, 1, 1), (7, 2, 2), (6, 2, 2), (6, 1, 4), (5, 4, 2), (5, 2, 3), (5, 1, 4),
+    (4, 4, 2), (4, 3, 2), (4, 2, 3), (4, 1, 4), (3, 3, 2), (3, 2, 3), (3, 1, 4), (2, 2, 3),
 )
 
 OFFSETS = ((0, 1), (-1, 0), (1, 1), (-1, 1), (1, 0), (0, -1), (1, -1), (-1, -1))
@@ -53,8 +54,14 @@
         lax.fori_loop(low, high, lambda i, c: (body(i), c)[1], 0)
 
 
+def schedule(A, B, C):
+    out = min(A, 3)
+    return dict(ahead=3, out=out, relay=out + 1, work=out + 2, merge=out + 3, hopf=1, hopb=1)
+
+
 def kernel(
     counts_abc,
+    plan,
     own, kv, pen, res,
     rcv11, rcv10, rcv01, out11, in11, out10, in10, out01, in01, held,
     ss11, rs11, ss10, rs10, ss01, rs01,
@@ -76,6 +83,10 @@
     for d in (zf, zb, xf, xb, z2f, z2b):
         pl.semaphore_signal(barrier, inc=1, device_id=d, device_id_type=MESH)
 
+    far_out, far_back = plan["hopf"], plan["hopb"]
+    lag = 2 if far_out else 3
+    last = lag + (3 if far_back else 4)
+
     def remote(src, dst, ssem, rsem, to):
         return pltpu.make_async_remote_copy(
             src_ref=src, dst_ref=dst, send_sem=ssem, recv_sem=rsem, device_id=to, device_id_type=MESH
@@ -83,16 +94,16 @@
 
     def copy11(e, t):
         src = (
-            own.at[t], rcv11.at[t, 0], rcv11.at[t, 1], own.at[t],
+            own.at[t], rcv11.at[t, 0], rcv11.at[t, 0 if far_out else 1], own.at[t],
             rcv11.at[t, 3], rcv11.at[t, 0], rcv11.at[t, 2], rcv11.at[t, 3],
         )[e]
-        to = (zf, zb, zf, zb, zf, xf, xf, xf)[e]
+        to = (zf, zb, z2b if far_out else zf, zb, zf, xf, xf, xf)[e]
         return remote(src, rcv11.at[t, e], ss11.at[t, e], rs11.at[t, e], to)
 
     def back11(i, t):
         if i == 0:
             return remote(out11.at[t, pl.ds(0, 3)], in11.at[t, pl.ds(0, 3)], ss11.at[t, 8], rs11.at[t, 8], xb)
-        to = {3: zf, 4: zf, 5: zb, 6: zf, 7: zb}[i]
+        to = {3: zf, 4: z2f if far_back else zf, 5: zb, 6: zf, 7: zb}[i]
         return remote(out11.at[t, i], in11.at[t, i], ss11.at[t, 6 + i], rs11.at[t, 6 + i], to)
 
     def copy10(e, t):
@@ -133,19 +144,24 @@
         blocks = [(own.at[t], None)] + [(rcv11.at[t, e], e) for e in range(8)]
         parts = compute(t, blocks)
         for e in range(8):
-            if TERM[e] < 4:
+            if TERM[e] < 4 or (far_back and TERM[e] == 5):
                 out11[t, TERM[e]] = parts[1 + e].astype(jnp.bfloat16)
             else:
                 held[t, TERM[e] - 4] = parts[1 + e]
         held[t, 4] = parts[0]
 
+    def plain(j):
+        res[j, 0] = compute(j, [(own.at[j], None)])[0].astype(jnp.bfloat16)
+
+    loop(A + B + C, HEADS, plain)
     pl.semaphore_wait(barrier, 6)
 
     def start11(t):
         copy11(0, t).start()
         copy11(3, t).start()
 
-    loop(0, A, start11)
+    ahead = min(A, plan["ahead"])
+    loop(0, ahead, start11)
 
     def others_out():
         def start10(t):
@@ -154,9 +170,6 @@
 
         loop(0, B, start10)
         loop(0, C, lambda t: copy01(0, t).start())
-
-    def plain(j):
-        res[j, 0] = compute(j, [(own.at[j], None)])[0].astype(jnp.bfloat16)
 
     def relay01(t):
         copy01(0, t).wait_recv()
@@ -187,51 +200,60 @@
         back01(0, t).start()
 
     def step(t):
+        if ahead < A:
+            @pl.when(t < A - ahead)
+            def _():
+                start11(t + ahead)
+
         @pl.when(t < A)
         def _():
             copy11(0, t).wait_recv()
+            if far_out:
+                copy11(2, t).start()
             copy11(1, t).start()
             copy11(5, t).start()
             copy11(3, t).wait_recv()
             copy11(4, t).start()
             copy11(7, t).start()
 
-        @pl.when(t == 0)
+        @pl.when(t == plan["out"])
         def _():
             others_out()
 
-        @pl.when((t >= 1) & (t < A + 1))
-        def _():
-            copy11(1, t - 1).wait_recv()
-            copy11(2, t - 1).start()
-
-        @pl.when((t >= 2) & (t < A + 2))
-        def _():
-            copy11(2, t - 2).wait_recv()
-            copy11(6, t - 2).start()
-
-        @pl.when(t == 2)
+        if not far_out:
+            @pl.when((t >= 1) & (t < A + 1))
+            def _():
+                copy11(1, t - 1).wait_recv()
+                copy11(2, t - 1).start()
+
+        @pl.when((t >= lag - 1) & (t < A + lag - 1))
+        def _():
+            copy11(2, t - lag + 1).wait_recv()
+            copy11(6, t - lag + 1).start()
+
+        @pl.when(t == plan["relay"])
         def _():
             loop(0, C, relay01)
-            loop(A + B + C, HEADS, plain)
-
-        @pl.when((t >= 3) & (t < A + 3))
-        def _():
-            u = t - 3
-            for e in (4, 5, 7, 6):
+
+        @pl.when((t >= lag) & (t < A + lag))
+        def _():
+            u = t - lag
+            for e in (1, 4, 5, 7, 6) if far_out else (4, 5, 7, 6):
                 copy11(e, u).wait_recv()
             attend11(u)
             back11(0, u).start()
             back11(3, u).start()
-
-        @pl.when(t == 3)
+            if far_back:
+                back11(5, u).start()
+
+        @pl.when(t == plan["work"])
         def _():
             loop(0, B, attend10)
             loop(0, C, attend01)
 
-        @pl.when((t >= 4) & (t < A + 4))
-        def _():
-            u = t - 4
+        @pl.when((t >= lag + 1) & (t < A + lag + 1))
+        def _():
+            u = t - lag - 1
             back11(0, u).wait_recv()
             out11[u, 4] = (held[u, 0] + f32(in11[u, 0])).astype(jnp.bfloat16)
             back11(4, u).start()
@@ -239,32 +261,37 @@
             out11[u, 7] = (held[u, 3] + f32(in11[u, 2]) + f32(in11[u, 3])).astype(jnp.bfloat16)
             back11(7, u).start()
 
-        @pl.when(t == 4)
+        @pl.when(t == plan["merge"])
         def _():
             loop(0, C, merge01)
 
-        @pl.when((t >= 5) & (t < A + 5))
-        def _():
-            u = t - 5
-            back11(4, u).wait_recv()
-            out11[u, 5] = (held[u, 1] + f32(in11[u, 4])).astype(jnp.bfloat16)
-            back11(5, u).start()
-
-        @pl.when((t >= 6) & (t < A + 6))
-        def _():
-            u = t - 6
+        if not far_back:
+            @pl.when((t >= lag + 2) & (t < A + lag + 2))
+            def _():
+                u = t - lag - 2
+                back11(4, u).wait_recv()
+                out11[u, 5] = (held[u, 1] + f32(in11[u, 4])).astype(jnp.bfloat16)
+                back11(5, u).start()
+
+        @pl.when((t >= last - 1) & (t < A + last - 1))
+        def _():
+            u = t - last + 1
+            term = held[u, 2] + f32(in11[u, 1])
             back11(5, u).wait_recv()
-            out11[u, 6] = (held[u, 2] + f32(in11[u, 1]) + f32(in11[u, 5])).astype(jnp.bfloat16)
+            if far_back:
+                back11(4, u).wait_recv()
+                term = term + f32(in11[u, 4])
+            out11[u, 6] = (term + f32(in11[u, 5])).astype(jnp.bfloat16)
             back11(6, u).start()
 
-        @pl.when(t >= 7)
-        def _():
-            u = t - 7
+        @pl.when(t >= last)
+        def _():
+            u = t - last
             back11(7, u).wait_recv()
             back11(6, u).wait_recv()
             res[u, 0] = (held[u, 4] + f32(in11[u, 6]) + f32(in11[u, 7])).astype(jnp.bfloat16)
 
-    loop(0, A + 7, step)
+    loop(0, A + last, step)
 
     def finish10(t):
         back10(0, t).wait_recv()
@@ -303,13 +330,23 @@
 
 def ordered(
     reach_ref, counts_ref, q_ref, k_ref, v_ref, o_ref, g_ref, lse_ref,
-    choice_ref, slot_ref, own, kv, pen, perm_ref,
+    choice_ref, slot_ref, own, kv, pen,
+    perm_ref, q_all, k_all, v_all, o_all, g_all, lse_all, stats, sems,
 ):
+    loads = [
+        pltpu.make_async_copy(src, dst, sems.at[i])
+        for i, (src, dst) in enumerate((
+            (lse_ref, lse_all), (g_ref.at[0, 0], g_all), (o_ref.at[0, 0], o_all),
+            (q_ref.at[0, 0], q_all), (k_ref.at[0, 0], k_all), (v_ref.at[0, 0], v_all),
+        ))
+    ]
+    for load in loads:
+        load.start()
     ta, ha = lax.axis_index("ta"), lax.axis_index("ha")
     s = 1 - 2 * lax.rem(ha, 2)
     live = counts_ref[ta, ha]
-    rt = [reach_ref[h, 0] for h in range(HEADS)]
-    rh = [reach_ref[h, 1] for h in range(HEADS)]
+    rt = [reach_ref[0, h] for h in range(HEADS)]
+    rh = [reach_ref[1, h] for h in range(HEADS)]
     n11 = sum(t * h for t, h in zip(rt, rh))
     n10 = sum(rt) - n11
     n01 = sum(rh) - n11
@@ -348,25 +385,39 @@
     keep = lax.broadcasted_iota(jnp.int32, (TOK, HEAD_DIM), 0) < live
     lane_ids = lax.broadcasted_iota(jnp.int32, (1, TOK), 1)
     sub_ids = lax.broadcasted_iota(jnp.int32, (8, TOK), 0)
+    for load in loads[:3]:
+        load.wait()
+    feature = lax.broadcasted_iota(jnp.int32, (16, HEADS * HEAD_DIM), 1) // HEAD_DIM
+    member = jnp.where(feature == lax.broadcasted_iota(jnp.int32, (16, HEADS * HEAD_DIM), 0), 1.0, 0.0)
+    member = member.astype(jnp.bfloat16)
+    prod = g_all[...].astype(jnp.float32) * o_all[...].astype(jnp.float32)
+    high = prod.astype(jnp.bfloat16)
+    low = (prod - high.astype(jnp.float32)).astype(jnp.bfloat16)
+    delta = nt(member, high) + nt(member, low)
+    delta_pieces = [p.astype(jnp.float32) for p in split3(delta)]
+    stats[...] = jnp.zeros_like(stats)
+    for h in range(HEADS):
+        lse_row = jnp.where(lane_ids < live, lse_all[h] * LOG2E, FAR)
+        for i, p in enumerate(split3(lse_row)):
+            stats[h, i:i + 1] = p.astype(jnp.float32)
+        for i, p in enumerate(delta_pieces):
+            stats[h, 3 + i:4 + i] = p[h:h + 1]
+    for load in loads[3:]:
+        load.wait()
     for j in range(HEADS):
         h = perm_ref[j]
         c = pl.ds(pl.multiple_of(h * HEAD_DIM, HEAD_DIM), HEAD_DIM)
-        g = g_ref[0, 0, :, c]
-        own[j, ROW_Q:ROW_Q + TOK] = q_ref[0, 0, :, c]
+        g = g_all[:, c]
+        own[j, ROW_Q:ROW_Q + TOK] = q_all[:, c]
         own[j, ROW_G:ROW_G + TOK] = g
-        kv[j, 0] = jnp.where(keep, k_ref[0, 0, :, c].astype(jnp.float32), 0.0).astype(jnp.bfloat16)
-        kv[j, 1] = v_ref[0, 0, :, c]
-        prod = g.astype(jnp.float32) * o_ref[0, 0, :, c].astype(jnp.float32)
-        delta_row = jnp.sum(prod.T, axis=0, keepdims=True)
-        lse_row = lse_ref[0, 0, pl.ds(h, 1), :] * LOG2E
-        rows = split3(jnp.where(lane_ids < live, lse_row, FAR)) + split3(delta_row)
-        rows = [r.astype(jnp.float32) for r in rows] + [jnp.zeros((10, TOK), jnp.float32)]
-        own[j, ROW_S:ROW_S + 16] = jnp.concatenate(rows, axis=0).astype(jnp.bfloat16)
+        kv[j, 0] = jnp.where(keep, k_all[:, c].astype(jnp.float32), 0.0).astype(jnp.bfloat16)
+        kv[j, 1] = v_all[:, c]
+        own[j, ROW_S:ROW_S + 16] = stats[h].astype(jnp.bfloat16)
         far = jnp.zeros((8, TOK), jnp.float32)
         for e, (dt, dh) in enumerate(OFFSETS):
             at, ah = ta + dt * s, ha + dh * s
             inside = (at >= 0) & (at < TILES_T) & (ah >= 0) & (ah < TILES_H)
-            seen = inside & (reach_ref[h, 0] >= abs(dt)) & (reach_ref[h, 1] >= abs(dh))
+            seen = inside & (reach_ref[0, h] >= abs(dt)) & (reach_ref[1, h] >= abs(dh))
             far = jnp.where(sub_ids == e, jnp.where(seen, jnp.float32(0.0), jnp.float32(FAR)), far)
         pen[j] = far
 
@@ -393,10 +444,11 @@
 
 def exchange(index, own, kv, pen):
     A, B, C = VARIANTS[index]
+    steps = schedule(A, B, C)
     dma = pltpu.SemaphoreType.DMA
     b, c = max(B, 1), max(C, 1)
     return pl.pallas_call(
-        functools.partial(kernel, (A, B, C)),
+        functools.partial(kernel, (A, B, C), steps),
         out_shape=jax.ShapeDtypeStruct((HEADS, 3, TOK, HEAD_DIM), jnp.bfloat16),
         in_specs=[VMEM] * 3,
         out_specs=VMEM,
@@ -431,12 +483,17 @@
             jax.ShapeDtypeStruct((HEADS, 2, TOK, HEAD_DIM), jnp.bfloat16),
             jax.ShapeDtypeStruct((HEADS, 8, TOK), jnp.float32),
         ),
-        in_specs=[SMEM] * 2 + [VMEM] * 6,
+        in_specs=[SMEM] * 2 + [pl.BlockSpec(memory_space=pl.ANY)] * 6,
         out_specs=(SMEM, SMEM, VMEM, VMEM, VMEM),
-        scratch_shapes=[pltpu.SMEM((HEADS,), jnp.int32)],
-        compiler_params=params,
+        scratch_shapes=[pltpu.SMEM((HEADS,), jnp.int32)]
+        + [pltpu.VMEM((TOK, HEADS * HEAD_DIM), jnp.bfloat16)] * 5
+        + [pltpu.VMEM((HEADS, 1, TOK), jnp.float32), pltpu.VMEM((HEADS, 16, TOK), jnp.float32), pltpu.SemaphoreType.DMA((6,))],
+        compiler_params=pltpu.CompilerParams(vmem_limit_bytes=60 * 2**20),
         name="ordered",
-    )(head_reach, tile_counts, queries, key_tiles, value_tiles, outputs, grads_out, log_sums)
+    )(
+        head_reach.T, tile_counts, queries, key_tiles, value_tiles, outputs, grads_out,
+        jnp.transpose(log_sums, (0, 2, 1, 3)).reshape(HEADS, 1, TOK),
+    )
     branches = [functools.partial(exchange, i) for i in range(len(VARIANTS))]
     res = branches[0](own, kv, pen) if len(branches) == 1 else lax.switch(choice[0], branches, own, kv, pen)
     tile = jax.ShapeDtypeStruct((1, 1, TOK, HEADS * HEAD_DIM), jnp.bfloat16)

time: 70.4 us -> 71.1 us (level)
  the two profiles are of different devices: /device:TPU:8 before, /device:TPU:40 now
where the time goes in v2:
time: 71.1 us; the launch traced here: 70.3 us
  Pallas kernels  68.2 us (96%)
  between operations  1.33 us (2%)
  loops' own time  0.76 us (1%)
    pallas_call x1, Pallas kernels, exchange(): pl.pallas_call(functools.partial(kernel, (A, B, C), steps), out_shape=jax...  63.3 us
    pallas_call x1, Pallas kernels, per_device(): pl.pallas_call(ordered, out_shape=(jax.ShapeDtypeStruct((1,), jnp.int32),...  3.2 us
    pallas_call x1, Pallas kernels, per_device(): pl.pallas_call(restored, out_shape=(tile, tile, tile), in_specs=[SMEM, SM...  1.73 us

profile of v2, /device:TPU:40, one launch (start us, length us, event | category | flops | bytes accessed | tf_op | source)
XLA Modules:
  0.0 70.3 jit_solution(3840476714139225114)
XLA Ops:
  0.6 3.2 %ordered.1 = (s32[1]{0:T(128)}, s32[12]{0:T(128)}, bf16[12,272,128]{2,1,0:T(8,128)(2,1)S(1)}, bf16[12,2,128,128]{3,2,1,0:T(8,128)(2,1)S(1)}, f32[12,8,128]{2,1,0:T(8,128)S(1)}) custom-call(s32[2,12]{1,0:T(2,128)} %bitcast.4, s32[4,8]{1,0:T(4,128)} %counts_ref.3, bf16[1,1,128,1536]{3,2,1,0:T(8,128)(2,1)} %q_ref.1, bf16[1,1,128,1536]{3,2,1,0:T(8,128)(2,1)} %k_ref.1, ...), custom_call_target="tpu_custom_call" | custom-call | tf_op jit(solution)/shard_map/ordered/pallas_call | solution.py:477
  4.5 0.0 copy-start
  4.5 0.0 copy-start.1
  4.5 64.1 %conditional.1 = (bf16[12,3,128,128]{3,2,1,0:T(8,128)(2,1)S(1)}) conditional(s32[]{:T(128)} %bitcast.2, (bf16[12,272,128]{2,1,0:T(8,128)(2,1)S(1)}, bf16[12,2,128,128]{3,2,1,0:T(8,128)(2,1)S(1)}, f32[12,8,128]{2,1,0:T(8,128)S(1)}) %tuple.55, (bf16[12,272,128]{2,1,0:T(8,128)(2,1)S(1)}, ...), branch_computations={%region_0.0_spmd, %region_1.0_spmd, %region_2.0_spmd, %region_3.0_... | conditional | bytes 8 | solution.py:498
  4.7 63.3 %exchange_5_1_4.1 = bf16[12,3,128,128]{3,2,1,0:T(8,128)(2,1)S(1)} custom-call(bf16[12,272,128]{2,1,0:T(8,128)(2,1)S(1)} %get-tuple-element.134.own, bf16[12,2,128,128]{3,2,1,0:T(8,128)(2,1)S(1)} %get-tuple-element.135.kv, f32[12,8,128]{2,1,0:T(8,128)S(1)} %get-tuple-element.136.pen), custom_call_target="tpu_custom_call" | custom-call | tf_op jit(solution)/shard_map/cond/branch_7_fun/exchange_5_1_4/pallas_call | solution.py:450
  68.6 0.0 copy-done
  68.6 0.0 copy-done.1
  68.6 1.7 %restored.1 = (bf16[1,1,128,1536]{3,2,1,0:T(8,128)(2,1)}, bf16[1,1,128,1536]{3,2,1,0:T(8,128)(2,1)}, bf16[1,1,128,1536]{3,2,1,0:T(8,128)(2,1)}) custom-call(s32[12]{0:T(128)S(1)} %copy-done.1, s32[4,8]{1,0:T(4,128)S(1)} %copy-done, bf16[12,3,128,128]{3,2,1,0:T(8,128)(2,1)S(1)} %get-tuple-element.174.res), custom_call_target="tpu_custom_call" | custom-call | tf_op jit(solution)/shard_map/restored/pallas_call | solution.py:500
Async XLA Ops:
  4.5 64.1 %copy-start = (s32[4,8]{1,0:T(4,128)S(1)}, s32[4,8]{1,0:T(4,128)}, u32[]{:S(2)}) copy-start(s32[4,8]{1,0:T(4,128)} %counts_ref.3) | copy-start | bytes 388
  4.5 64.1 %copy-start.1 = (s32[12]{0:T(128)S(1)}, s32[12]{0:T(128)}, u32[]{:S(2)}) copy-start(s32[12]{0:T(128)} %get-tuple-element.169.slot_ref) | copy-start | bytes 148

commit v3 on v2

v3 whole, which is shorter than its diff:
```python
import functools
import math

import jax
import jax.numpy as jnp
from jax import lax
from jax.experimental import pallas as pl
from jax.experimental.pallas import tpu as pltpu
from jax.sharding import PartitionSpec as P

HEADS = 12
OUT01 = 1
HEAD_DIM = 128
TOK = 128
TILES_T = 4
TILES_H = 8
MESH = pl.DeviceIdType.MESH
FAR = 1e30
LOG2E = math.log2(math.e)
SCALE = HEAD_DIM ** (-0.5)

ROW_Q, ROW_G, ROW_S, ROWS = 0, 128, 256, 272

VARIANTS = (
    (12, 0), (9, 2), (8, 2), (7, 4), (7, 2), (6, 4), (6, 3), (6, 2), (5, 4), (5, 2), (4, 4), (4, 2),
)

PAIRS = (
    ((-1, 1), (-1, 1)), ((-1, 0), (-1, 0)), ((-1, -1), (-1, -1)),
    ((0, 0), (0, -1)), ((-1, 1), (-1, 0)), ((-1, 0), (-1, -1)), ((0, 2), (0, 1)), ((-1, 2), (-1, 1)),
    ((0, 1), (0, 1)), ((0, -1), (0, -1)),
)
PEN_ROWS = 16


def nt(a, b):
    return lax.dot_general(a, b, (((1,), (1,)), ((), ())), preferred_element_type=jnp.float32)


def nn(a, b):
    return jnp.dot(a, b, preferred_element_type=jnp.float32)


def tn(a, b):
    return lax.dot_general(a, b, (((0,), (0,)), ((), ())), preferred_element_type=jnp.float32)


def split3(x):
    hi = x.astype(jnp.bfloat16)
    rest = x - hi.astype(jnp.float32)
    mid = rest.astype(jnp.bfloat16)
    lo = (rest - mid.astype(jnp.float32)).astype(jnp.bfloat16)
    return [hi, mid, lo]


def loop(low, high, body):
    if high > low:
        lax.fori_loop(low, high, lambda i, c: (body(i), c)[1], 0)


def kernel(
    counts,
    own, kv, pen, res,
    rkv, rq, rq01, oq, iq, ogr, igr, o01, i01, held,
    ss, rs, ss01, rs01,
):
    A, C = counts
    grp, ta, ha = lax.axis_index("grp"), lax.axis_index("ta"), lax.axis_index("ha")
    x, p = ha // 2, lax.rem(ha, 2)
    z = ta * 2 + p
    s = 1 - 2 * p

    def dev(dx, dz):
        zz = lax.rem(z + dz * s + 8, 8)
        xx = lax.rem(x + dx * s + 4, 4)
        return (grp, zz // 2, xx * 2 + lax.rem(zz, 2))

    zf, zb, xf, xb, z2f, z2b = dev(0, 1), dev(0, -1), dev(1, 0), dev(-1, 0), dev(0, 2), dev(0, -2)

    barrier = pltpu.get_barrier_semaphore()
    for d in (zf, zb, xf, xb, z2f, z2b):
        pl.semaphore_signal(barrier, inc=1, device_id=d, device_id_type=MESH)

    def remote(src, dst, ssem, rsem, to):
        return pltpu.make_async_remote_copy(
            src_ref=src, dst_ref=dst, send_sem=ssem, recv_sem=rsem, device_id=to, device_id_type=MESH
        )

    def copy(i, t):
        src, dst, to = (
            (kv.at[t], rkv.at[t], zf),
            (own.at[t], rq.at[t, 0], zb),
            (own.at[t], rq.at[t, 1], z2f),
            (own.at[t], rq.at[t, 2], xb),
            (rq.at[t, 1], rq.at[t, 3], xb),
            (rq.at[t, 0], rq.at[t, 4], xf),
        )[i]
        return remote(src, dst, ss.at[t, i], rs.at[t, i], to)

    def back(i, t):
        src, dst, to = (
            (oq.at[t, pl.ds(0, 2)], iq.at[t, pl.ds(0, 2)], xf),
            (oq.at[t, 2], iq.at[t, 2], xb),
            (oq.at[t, 3], iq.at[t, 3], zb),
            (oq.at[t, 4], iq.at[t, 4], z2b),
            (ogr.at[t], igr.at[t], zf),
        )[i]
        return remote(src, dst, ss.at[t, 6 + i], rs.at[t, 6 + i], to)

    def copy01(e, t):
        src = own.at[A + t] if e == 0 else rq01.at[t, 0]
        return remote(src, rq01.at[t, e], ss01.at[t, e], rs01.at[t, e], (zf, xf)[e])

    def back01(e, t):
        return remote(o01.at[t, e], i01.at[t, e], ss01.at[t, 2 + e], rs01.at[t, 2 + e], (zf, xb)[e])

    def attend(j, keys, blocks):
        k0, v0 = keys[0], keys[1]
        lse_rows, delta_rows = [], []
        for ref, row in blocks:
            rows = ref[ROW_S:ROW_S + 16].astype(jnp.float32)
            lse_row = rows[0:1] + rows[1:2] + rows[2:3]
            lse_rows.append(lse_row if row is None else lse_row + pen[j, row:row + 1])
            delta_rows.append(rows[3:4] + rows[4:5] + rows[5:6])
        qs = jnp.concatenate([ref[ROW_Q:ROW_Q + TOK] for ref, _ in blocks], axis=0)
        gs = jnp.concatenate([ref[ROW_G:ROW_G + TOK] for ref, _ in blocks], axis=0)
        lse_row, delta_row = jnp.concatenate(lse_rows, axis=1), jnp.concatenate(delta_rows, axis=1)
        prob = jnp.exp2(nt(k0, qs) * (SCALE * LOG2E) - lse_row)
        ds = (prob * (nt(v0, gs) - delta_row) * SCALE).astype(jnp.bfloat16)
        dv = nn(prob.astype(jnp.bfloat16), gs)
        dk = nn(ds, qs)
        dq = tn(ds, k0)
        return dk, dv, [dq[i * TOK:(i + 1) * TOK] for i in range(len(blocks))]

    def bf16(v):
        return v.astype(jnp.bfloat16)

    def f32(v):
        return v.astype(jnp.float32)

    def plain(j):
        dk, dv, dq = attend(j, kv.at[j], [(own.at[j], None)])
        res[j, 0], res[j, 1], res[j, 2] = bf16(dq[0]), bf16(dk), bf16(dv)

    loop(A + C, HEADS, plain)
    pl.semaphore_wait(barrier, 6)

    def start(t):
        for i in (2, 1, 0, 3):
            copy(i, t).start()

    def relay01(t):
        copy01(0, t).wait_recv()
        copy01(1, t).start()

    def attend01(t):
        copy01(1, t).wait_recv()
        j = A + t
        dk, dv, dq = attend(j, kv.at[j], [(own.at[j], None), (rq01.at[t, 0], 8), (rq01.at[t, 1], 9)])
        res[j, 1], res[j, 2] = bf16(dk), bf16(dv)
        o01[t, 1] = bf16(dq[2])
        back01(1, t).start()
        held[j, 0] = dq[0]
        held[j, 1] = dq[1]

    def merge01(t):
        back01(1, t).wait_recv()
        o01[t, 0] = bf16(held[A + t, 1] + f32(i01[t, 1]))
        back01(0, t).start()

    ahead = min(A, 2 if A > 4 else 3)
    loop(0, ahead, start)

    def step(t):
        if ahead < A:
            @pl.when(t < A - ahead)
            def _():
                start(t + ahead)

        @pl.when(t < A)
        def _():
            copy(2, t).wait_recv()
            copy(4, t).start()
            copy(1, t).wait_recv()
            copy(5, t).start()

        @pl.when(t == OUT01)
        def _():
            loop(0, C, lambda i: copy01(0, i).start())

        @pl.when(t == OUT01 + 1)
        def _():
            loop(0, C, relay01)

        @pl.when((t >= 1) & (t < A + 1))
        def _():
            u = t - 1
            for i in (0, 3, 5, 4):
                copy(i, u).wait_recv()
            tiles = [rq.at[u, i] for i in range(5)]
            dk, dv, dq = attend(
                u, rkv.at[u],
                [(own.at[u], 3), (tiles[0], 4), (tiles[1], 5), (tiles[2], 6), (tiles[3], 7)],
            )
            oq[u, 0] = bf16(dq[3])
            oq[u, 1] = bf16(dq[4])
            back(0, u).start()
            ogr[u, 0] = bf16(dk)
            ogr[u, 1] = bf16(dv)
            back(4, u).start()
            for i in range(3):
                held[u, i] = dq[i]
            dk, dv, dq = attend(
                u, kv.at[u], [(own.at[u], None), (tiles[0], 0), (tiles[1], 1), (tiles[4], 2)]
            )
            oq[u, 2] = bf16(dq[3])
            back(1, u).start()
            for i in range(3):
                held[u, i] = held[u, i] + dq[i]
            held[u, 3] = dk
            held[u, 4] = dv

        @pl.when(t == OUT01 + 2)
        def _():
            loop(0, C, attend01)

        @pl.when((t >= 2) & (t < A + 2))
        def _():
            u = t - 2
            back(0, u).wait_recv()
            oq[u, 4] = bf16(held[u, 2] + f32(iq[u, 1]))
            back(3, u).start()
            back(1, u).wait_recv()
            oq[u, 3] = bf16(held[u, 1] + f32(iq[u, 2]))
            back(2, u).start()

        @pl.when(t == OUT01 + 3)
        def _():
            loop(0, C, merge01)

        @pl.when(t >= 3)
        def _():
            u = t - 3
            back(4, u).wait_recv()
            res[u, 1] = bf16(held[u, 3] + f32(igr[u, 0]))
            res[u, 2] = bf16(held[u, 4] + f32(igr[u, 1]))
            back(2, u).wait_recv()
            back(3, u).wait_recv()
            res[u, 0] = bf16(held[u, 0] + f32(iq[u, 0]) + f32(iq[u, 3]) + f32(iq[u, 4]))

    loop(0, A + 3, step)

    def finish01(t):
        back01(0, t).wait_recv()
        res[A + t, 0] = bf16(held[A + t, 0] + f32(i01[t, 0]))

    loop(0, C, finish01)

    def drain(t):
        for i in range(6):
            copy(i, t).wait_send()
        for i in range(5):
            back(i, t).wait_send()

    def drain01(t):
        for e in range(2):
            copy01(e, t).wait_send()
            back01(e, t).wait_send()

    loop(0, A, drain)
    loop(0, C, drain01)


def ordered(
    reach_ref, counts_ref, q_ref, k_ref, v_ref, o_ref, g_ref, lse_ref,
    choice_ref, slot_ref, own, kv, pen,
    perm_ref, q_all, k_all, v_all, o_all, g_all, lse_all, stats, sems,
):
    loads = [
        pltpu.make_async_copy(src, dst, sems.at[i])
        for i, (src, dst) in enumerate((
            (lse_ref, lse_all), (g_ref.at[0, 0], g_all), (o_ref.at[0, 0], o_all),
            (q_ref.at[0, 0], q_all), (k_ref.at[0, 0], k_all), (v_ref.at[0, 0], v_all),
        ))
    ]
    for load in loads:
        load.start()
    ta, ha = lax.axis_index("ta"), lax.axis_index("ha")
    s = 1 - 2 * lax.rem(ha, 2)
    live = counts_ref[ta, ha]
    rt = [reach_ref[0, h] for h in range(HEADS)]
    rh = [reach_ref[1, h] for h in range(HEADS)]
    n1 = sum(rt)
    n01 = sum(rh) - sum(t * h for t, h in zip(rt, rh))
    choice, A, C = [jnp.int32(v) for v in (0, *VARIANTS[0])]
    for i in sorted(range(len(VARIANTS)), key=lambda i: -price(VARIANTS[i])):
        a, c = VARIANTS[i]
        fits = n1 + jnp.maximum(n01 - c, 0) <= a
        choice, A, C = [jnp.where(fits, new, old) for new, old in zip((i, a, c), (choice, A, C))]
    choice_ref[0] = choice
    c1, c01, c00 = [jnp.int32(0)] * 3
    first = []
    for h in range(HEADS):
        own01 = (rt[h] == 0) & (rh[h] == 1) & (c01 < C)
        none = (rt[h] == 0) & (rh[h] == 0)
        first.append(jnp.where(none, -1, jnp.where(own01, A + c01, c1)))
        c01 = c01 + jnp.where(own01, 1, 0)
        c1 = c1 + jnp.where(own01 | none, 0, 1)
    for h in range(HEADS):
        none = first[h] < 0
        in1 = none & (c1 < A)
        in01 = none & (c1 >= A) & (c01 < C)
        in00 = none & (c1 >= A) & (c01 >= C)
        slot = jnp.where(none, jnp.where(in1, c1, jnp.where(in01, A + c01, A + C + c00)), first[h])
        c1, c01, c00 = [n + jnp.where(taken, 1, 0) for n, taken in ((c1, in1), (c01, in01), (c00, in00))]
        slot_ref[h] = slot
        perm_ref[slot] = h
    keep = lax.broadcasted_iota(jnp.int32, (TOK, HEAD_DIM), 0) < live
    lane_ids = lax.broadcasted_iota(jnp.int32, (1, TOK), 1)
    sub_ids = lax.broadcasted_iota(jnp.int32, (PEN_ROWS, TOK), 0)
    for load in loads[:3]:
        load.wait()
    feature = lax.broadcasted_iota(jnp.int32, (16, HEADS * HEAD_DIM), 1) // HEAD_DIM
    member = jnp.where(feature == lax.broadcasted_iota(jnp.int32, (16, HEADS * HEAD_DIM), 0), 1.0, 0.0)
    member = member.astype(jnp.bfloat16)
    prod = g_all[...].astype(jnp.float32) * o_all[...].astype(jnp.float32)
    high = prod.astype(jnp.bfloat16)
    low = (prod - high.astype(jnp.float32)).astype(jnp.bfloat16)
    delta = nt(member, high) + nt(member, low)
    delta_pieces = [p.astype(jnp.float32) for p in split3(delta)]
    stats[...] = jnp.zeros_like(stats)
    for h in range(HEADS):
        lse_row = jnp.where(lane_ids < live, lse_all[h] * LOG2E, FAR)
        for i, p in enumerate(split3(lse_row)):
            stats[h, i:i + 1] = p.astype(jnp.float32)
        for i, p in enumerate(delta_pieces):
            stats[h, 3 + i:4 + i] = p[h:h + 1]
    for load in loads[3:]:
        load.wait()
    for j in range(HEADS):
        h = perm_ref[j]
        c = pl.ds(pl.multiple_of(h * HEAD_DIM, HEAD_DIM), HEAD_DIM)
        g = g_all[:, c]
        own[j, ROW_Q:ROW_Q + TOK] = q_all[:, c]
        own[j, ROW_G:ROW_G + TOK] = g
        kv[j, 0] = jnp.where(keep, k_all[:, c].astype(jnp.float32), 0.0).astype(jnp.bfloat16)
        kv[j, 1] = v_all[:, c]
        own[j, ROW_S:ROW_S + 16] = stats[h].astype(jnp.bfloat16)
        far = jnp.zeros((PEN_ROWS, TOK), jnp.float32)
        for e, ((at, ah), (dt, dh)) in enumerate(PAIRS):
            at, ah = ta + at * s, ha + ah * s
            inside = (at >= 0) & (at < TILES_T) & (ah >= 0) & (ah < TILES_H)
            seen = inside & (reach_ref[0, h] >= abs(dt)) & (reach_ref[1, h] >= abs(dh))
            far = jnp.where(sub_ids == e, jnp.where(seen, jnp.float32(0.0), jnp.float32(FAR)), far)
        pen[j] = far


def restored(slot_ref, counts_ref, res, dq_ref, dk_ref, dv_ref):
    live = counts_ref[lax.axis_index("ta"), lax.axis_index("ha")]
    keep = lax.broadcasted_iota(jnp.int32, (TOK, HEAD_DIM), 0) < live
    for h in range(HEADS):
        j = slot_ref[h]
        c = slice(h * HEAD_DIM, (h + 1) * HEAD_DIM)
        dq_ref[0, 0, :, c] = res[j, 0]
        for i, out in ((1, dk_ref), (2, dv_ref)):
            out[0, 0, :, c] = jnp.where(keep, res[j, i].astype(jnp.float32), 0.0).astype(jnp.bfloat16)


def price(variant):
    A, C = variant
    return 7 * A + 3 * C


VMEM, SMEM = pl.BlockSpec(memory_space=pltpu.VMEM), pl.BlockSpec(memory_space=pltpu.SMEM)
OWN = (HEADS, ROWS, HEAD_DIM)


def exchange(index, own, kv, pen):
    A, C = VARIANTS[index]
    dma, c = pltpu.SemaphoreType.DMA, max(C, 1)

    def terms(*lead):
        return pltpu.VMEM((*lead, TOK, HEAD_DIM), jnp.bfloat16)

    return pl.pallas_call(
        functools.partial(kernel, (A, C)),
        out_shape=jax.ShapeDtypeStruct((HEADS, 3, TOK, HEAD_DIM), jnp.bfloat16),
        in_specs=[VMEM] * 3,
        out_specs=VMEM,
        scratch_shapes=[
            terms(A, 2),
            pltpu.VMEM((A, 5, ROWS, HEAD_DIM), jnp.bfloat16),
            pltpu.VMEM((c, 2, ROWS, HEAD_DIM), jnp.bfloat16),
            terms(A, 5), terms(A, 5), terms(A, 2), terms(A, 2), terms(c, 2), terms(c, 2),
            pltpu.VMEM((HEADS, 5, TOK, HEAD_DIM), jnp.float32),
            dma((A, 11)), dma((A, 11)), dma((c, 4)), dma((c, 4)),
        ],
        compiler_params=pltpu.CompilerParams(
            collective_id=index, has_side_effects=True, vmem_limit_bytes=56 * 2**20
        ),
        name=f"exchange_{A}_{C}",
    )(own, kv, pen)


def per_device(queries, key_tiles, value_tiles, outputs, grads_out, log_sums, tile_counts, head_reach):
    params = pltpu.CompilerParams(vmem_limit_bytes=32 * 2**20)
    choice, slots, own, kv, pen = pl.pallas_call(
        ordered,
        out_shape=(
            jax.ShapeDtypeStruct((1,), jnp.int32),
            jax.ShapeDtypeStruct((HEADS,), jnp.int32),
            jax.ShapeDtypeStruct(OWN, jnp.bfloat16),
            jax.ShapeDtypeStruct((HEADS, 2, TOK, HEAD_DIM), jnp.bfloat16),
            jax.ShapeDtypeStruct((HEADS, PEN_ROWS, TOK), jnp.float32),
        ),
        in_specs=[SMEM] * 2 + [pl.BlockSpec(memory_space=pl.ANY)] * 6,
        out_specs=(SMEM, SMEM, VMEM, VMEM, VMEM),
        scratch_shapes=[pltpu.SMEM((HEADS,), jnp.int32)]
        + [pltpu.VMEM((TOK, HEADS * HEAD_DIM), jnp.bfloat16)] * 5
        + [pltpu.VMEM((HEADS, 1, TOK), jnp.float32), pltpu.VMEM((HEADS, 16, TOK), jnp.float32), pltpu.SemaphoreType.DMA((6,))],
        compiler_params=pltpu.CompilerParams(vmem_limit_bytes=60 * 2**20),
        name="ordered",
    )(
        head_reach.T, tile_counts, queries, key_tiles, value_tiles, outputs, grads_out,
        jnp.transpose(log_sums, (0, 2, 1, 3)).reshape(HEADS, 1, TOK),
    )
    branches = [functools.partial(exchange, i) for i in range(len(VARIANTS))]
    res = branches[0](own, kv, pen) if len(branches) == 1 else lax.switch(choice[0], branches, own, kv, pen)
    tile = jax.ShapeDtypeStruct((1, 1, TOK, HEADS * HEAD_DIM), jnp.bfloat16)
    return pl.pallas_call(
        restored,
        out_shape=(tile, tile, tile),
        in_specs=[SMEM, SMEM, VMEM],
        out_specs=(VMEM, VMEM, VMEM),
        compiler_params=params,
        name="restored",
    )(slots, tile_counts, res)


def solution(mesh):
    tiles = P(("grp", "ta"), "ha", None, None)
    return jax.shard_map(
        per_device, mesh=mesh,
        in_specs=(tiles,) * 6 + (P("grp", None), P()),
        out_specs=(tiles,) * 3, check_vma=False,
    )
```

time: 71.1 us -> 59.6 us (0.84)
  the two profiles are of different devices: /device:TPU:40 before, /device:TPU:48 now
where the time goes in v3:
time: 59.6 us; the launch traced here: 59.4 us
  Pallas kernels  57.3 us (96%)
  between operations  1.33 us (2%)
  loops' own time  0.77 us (1%)
    pallas_call x1, Pallas kernels, exchange(): pl.pallas_call(functools.partial(kernel, (A, C)), out_shape=jax.ShapeDtyp...  52.3 us
    pallas_call x1, Pallas kernels, per_device(): pl.pallas_call(ordered, out_shape=(jax.ShapeDtypeStruct((1,), jnp.int32),...  3.25 us
    pallas_call x1, Pallas kernels, per_device(): pl.pallas_call(restored, out_shape=(tile, tile, tile), in_specs=[SMEM, SM...  1.73 us

profile of v3, /device:TPU:48, one launch (start us, length us, event | category | flops | bytes accessed | tf_op | source)
XLA Modules:
  0.0 59.4 jit_solution(5305097490658481386)
XLA Ops:
  0.6 3.3 %ordered.1 = (s32[1]{0:T(128)}, s32[12]{0:T(128)}, bf16[12,272,128]{2,1,0:T(8,128)(2,1)S(1)}, bf16[12,2,128,128]{3,2,1,0:T(8,128)(2,1)S(1)}, f32[12,16,128]{2,1,0:T(8,128)S(1)}) custom-call(s32[2,12]{1,0:T(2,128)} %bitcast.4, s32[4,8]{1,0:T(4,128)} %counts_ref.3, bf16[1,1,128,1536]{3,2,1,0:T(8,128)(2,1)} %q_ref.1, bf16[1,1,128,1536]{3,2,1,0:T(8,128)(2,1)} %k_ref.1, ...), custom_call_target="tpu_custom_call" | custom-call | tf_op jit(solution)/shard_map/ordered/pallas_call | solution.py:407
  4.5 0.0 copy-start
  4.6 0.0 copy-start.1
  4.6 53.1 %conditional.1 = (bf16[12,3,128,128]{3,2,1,0:T(8,128)(2,1)S(1)}) conditional(s32[]{:T(128)} %bitcast.2, (bf16[12,272,128]{2,1,0:T(8,128)(2,1)S(1)}, bf16[12,2,128,128]{3,2,1,0:T(8,128)(2,1)S(1)}, f32[12,16,128]{2,1,0:T(8,128)S(1)}) %tuple.43, (bf16[12,272,128]{2,1,0:T(8,128)(2,1)S(1)}, ...), branch_computations={%region_0.0_spmd, %region_1.0_spmd, %region_2.0_spmd, %region_3.0_... | conditional | bytes 8 | solution.py:428
  4.8 52.3 %exchange_6_2.1 = bf16[12,3,128,128]{3,2,1,0:T(8,128)(2,1)S(1)} custom-call(bf16[12,272,128]{2,1,0:T(8,128)(2,1)S(1)} %get-tuple-element.106.own, bf16[12,2,128,128]{3,2,1,0:T(8,128)(2,1)S(1)} %get-tuple-element.107.kv, f32[12,16,128]{2,1,0:T(8,128)S(1)} %get-tuple-element.108.pen), custom_call_target="tpu_custom_call" | custom-call | tf_op jit(solution)/shard_map/cond/branch_7_fun/exchange_6_2/pallas_call | solution.py:385
  57.7 0.0 copy-done
  57.7 0.0 copy-done.1
  57.7 1.7 %restored.1 = (bf16[1,1,128,1536]{3,2,1,0:T(8,128)(2,1)}, bf16[1,1,128,1536]{3,2,1,0:T(8,128)(2,1)}, bf16[1,1,128,1536]{3,2,1,0:T(8,128)(2,1)}) custom-call(s32[12]{0:T(128)S(1)} %copy-done.1, s32[4,8]{1,0:T(4,128)S(1)} %copy-done, bf16[12,3,128,128]{3,2,1,0:T(8,128)(2,1)S(1)} %get-tuple-element.134.res), custom_call_target="tpu_custom_call" | custom-call | tf_op jit(solution)/shard_map/restored/pallas_call | solution.py:430
Async XLA Ops:
  4.5 53.1 %copy-start = (s32[4,8]{1,0:T(4,128)S(1)}, s32[4,8]{1,0:T(4,128)}, u32[]{:S(2)}) copy-start(s32[4,8]{1,0:T(4,128)} %counts_ref.3) | copy-start | bytes 388
  4.6 53.1 %copy-start.1 = (s32[12]{0:T(128)S(1)}, s32[12]{0:T(128)}, u32[]{:S(2)}) copy-start(s32[12]{0:T(128)} %get-tuple-element.129.slot_ref) | copy-start | bytes 148
